TPU v7x, 32 devices: a whole 2x2x4 slice. The times are simulated.
32 devices in a mesh: dp: 16 (over z, x, core), seq: 2 (over y).
Axes of the slice: x: 2, y: 2, z: 4, core: 2. Of those that a mesh axis runs over, the one named last changes fastest.
Arguments:
- inputs: float32 [16, 1024, 1088], P('dp', 'seq'), may hold values from -6 to 6
- attend_weight: float32 [1088, 3264], P('dp', 'seq'), may hold values from -0.1875 to 0.1875
- out_weight: float32 [1088, 1088], P('dp', 'seq'), may hold values from -0.75 to 0.75
- up_weight: float32 [1088, 4352], P('dp', 'seq'), may hold values from -0.1875 to 0.1875
- down_weight: float32 [4352, 1088], P('dp', 'seq'), may hold values from -0.09375 to 0.09375
- vectors: float32 [1088, 8], P('dp', 'seq'), may hold values from -1.2 to 1.6
- up_bias: float32 [4352], P(('dp', 'seq')), may hold values from -3 to 3
- cotangent: float32 [16, 1024, 1088], P('dp', 'seq'), may hold values from -6 to 6
Outputs:
- outputs: float32 [16, 1024, 1088], P('dp', 'seq')
- grad_inputs: float32 [16, 1024, 1088], P('dp', 'seq')
- grad_attend: float32 [1088, 3264], P('dp', 'seq')
- grad_out: float32 [1088, 1088], P('dp', 'seq')
- grad_up: float32 [1088, 4352], P('dp', 'seq')
- grad_down: float32 [4352, 1088], P('dp', 'seq')
- grad_vectors: float32 [1088, 8], P('dp', 'seq')
- grad_up_bias: float32 [4352], P(('dp', 'seq'))
All inputs are finite; a program needn't handle non-finite values.
Results may differ from a plain program's by a relative error of at most 0.012.
Values may be sent and summed in bfloat16 or wider, within the bound.
A program may use at most 320 MiB of HBM per device.

v0:
```python
import math

import jax
import jax.numpy as jnp
from jax import lax
from jax.sharding import PartitionSpec as P

HEADS = 17


def layer_norm(values, gain_vec, bias_vec):
    center = values - jnp.mean(values, -1, keepdims=True)
    spread = jnp.mean(center * center, -1, keepdims=True)
    return center * lax.rsqrt(spread + 1e-05) * gain_vec + bias_vec


def gelu_exact(values):
    return jax.nn.gelu(values, approximate=False)


def masked_scores(query_rows, key_rows, query_pos, key_pos, score_scale):
    allowed = key_pos[None, :] <= query_pos[:, None]
    scores = (
        jnp.einsum("bqhe,bkhe->bhqk", query_rows, key_rows, preferred_element_type=jnp.float32)
        * score_scale
    )
    return jnp.where(allowed[None, None], scores, -1e30)


def attend_forward(query_rows, key_rows, value_rows, query_pos, score_scale):
    key_pos = jnp.arange(key_rows.shape[1])
    scores = masked_scores(query_rows, key_rows, query_pos, key_pos, score_scale)
    top_score = jnp.max(scores, -1, keepdims=True)
    raised = jnp.exp(scores - top_score)
    totals = jnp.sum(raised, -1, keepdims=True)
    attn_probs = (raised / totals).astype(jnp.bfloat16)
    mixed_attention = jnp.einsum(
        "bhqk,bkhe->bqhe", attn_probs, value_rows, preferred_element_type=jnp.float32
    )
    return (mixed_attention, top_score + jnp.log(totals))


def score_grads(query_rows, key_rows, value_rows, grad_mixed, log_total, query_pos, score_scale):
    key_pos = jnp.arange(key_rows.shape[1])
    scores = masked_scores(query_rows, key_rows, query_pos, key_pos, score_scale)
    attn_probs = jnp.exp(scores - log_total)
    grad_probs = jnp.einsum(
        "bqhe,bkhe->bhqk", grad_mixed, value_rows, preferred_element_type=jnp.float32
    )
    row_dot = jnp.sum(grad_probs * attn_probs, -1, keepdims=True)
    grad_scores = (attn_probs * (grad_probs - row_dot)).astype(jnp.bfloat16)
    return (attn_probs, grad_scores, row_dot)


def query_backward(query_rows, key_rows, value_rows, grad_mixed, log_total, query_pos, score_scale):
    attn_probs, grad_scores, row_dot = score_grads(
        query_rows, key_rows, value_rows, grad_mixed, log_total, query_pos, score_scale
    )
    grad_query = (
        jnp.einsum("bhqk,bkhe->bqhe", grad_scores, key_rows, preferred_element_type=jnp.float32)
        * score_scale
    )
    return (grad_query, row_dot)


def body(inputs, attend_weight, out_weight, up_weight, down_weight, vectors, up_bias, cotangent):
    seq_count, piece_rows, model_width = inputs.shape
    head_dim = model_width // HEADS
    score_scale = 1.0 / math.sqrt(head_dim)
    seq_attend, seq_out, seq_up, seq_down, seq_vec, seq_bias = (
        lax.all_gather(attend_weight.astype(jnp.bfloat16), "seq", axis=1, tiled=True),
        lax.all_gather(out_weight.astype(jnp.bfloat16), "seq", axis=1, tiled=True),
        lax.all_gather(up_weight.astype(jnp.bfloat16), "seq", axis=1, tiled=True),
        lax.all_gather(down_weight.astype(jnp.bfloat16), "seq", axis=1, tiled=True),
        lax.all_gather(vectors.astype(jnp.bfloat16), "seq", axis=1, tiled=True),
        lax.all_gather(up_bias.astype(jnp.bfloat16), "seq", axis=0, tiled=True),
    )
    full_attend, full_out, full_up, full_down, full_vec, full_bias = (
        lax.all_gather(seq_attend, "dp", axis=0, tiled=True),
        lax.all_gather(seq_out, "dp", axis=0, tiled=True),
        lax.all_gather(seq_up, "dp", axis=0, tiled=True),
        lax.all_gather(seq_down, "dp", axis=0, tiled=True),
        lax.all_gather(seq_vec, "dp", axis=0, tiled=True),
        lax.all_gather(seq_bias, "dp", axis=0, tiled=True),
    )
    column_total = full_vec.astype(jnp.float32)
    up_projection_bias = full_bias.astype(jnp.float32)
    first_normed = layer_norm(inputs, column_total[:, 0], column_total[:, 1]).astype(jnp.bfloat16)
    projected_output = jnp.einsum(
        "spd,de->spe", first_normed, full_attend, preferred_element_type=jnp.float32
    )
    query_rows = (projected_output[..., :model_width] + column_total[:, 2]).astype(jnp.bfloat16)
    key_rows = projected_output[..., model_width : 2 * model_width].astype(jnp.bfloat16)
    value_rows = (projected_output[..., 2 * model_width :] + column_total[:, 3]).astype(
        jnp.bfloat16
    )
    key_all, value_all = (
        lax.all_gather(key_rows, "seq", axis=1, tiled=True),
        lax.all_gather(value_rows, "seq", axis=1, tiled=True),
    )
    length = key_all.shape[1]
    own_start = lax.axis_index("seq") * piece_rows
    query_pos = own_start + jnp.arange(piece_rows)
    per_block = math.gcd(seq_count, max(1, 512 // piece_rows))
    blocks = seq_count // per_block

    def blocked(stacked, row_count):
        return stacked.reshape(blocks, per_block, row_count, HEADS, head_dim)

    query_blk = blocked(query_rows, piece_rows)
    key_blk = blocked(key_all, length)
    value_blk = blocked(value_all, length)

    def forward_block(operands):
        return attend_forward(operands[0], operands[1], operands[2], query_pos, score_scale)

    mixed_blk, log_total = lax.map(forward_block, (query_blk, key_blk, value_blk))
    mixed_low = mixed_blk.reshape(seq_count, piece_rows, model_width).astype(jnp.bfloat16)
    middle_hidden = (
        inputs
        + jnp.einsum("spd,de->spe", mixed_low, full_out, preferred_element_type=jnp.float32)
        + column_total[:, 4]
    )
    second_normed = layer_norm(middle_hidden, column_total[:, 5], column_total[:, 6]).astype(
        jnp.bfloat16
    )
    hidden_before_gelu = (
        jnp.einsum("spd,df->spf", second_normed, full_up, preferred_element_type=jnp.float32)
        + up_projection_bias
    )
    gelu_output = gelu_exact(hidden_before_gelu).astype(jnp.bfloat16)
    outputs = (
        middle_hidden
        + jnp.einsum("spf,fd->spd", gelu_output, full_down, preferred_element_type=jnp.float32)
        + column_total[:, 7]
    )
    again_attend, again_out, again_up, again_down = (
        lax.all_gather(attend_weight.astype(jnp.bfloat16), "seq", axis=1, tiled=True),
        lax.all_gather(out_weight.astype(jnp.bfloat16), "seq", axis=1, tiled=True),
        lax.all_gather(up_weight.astype(jnp.bfloat16), "seq", axis=1, tiled=True),
        lax.all_gather(down_weight.astype(jnp.bfloat16), "seq", axis=1, tiled=True),
    )
    back_attend, back_out, back_up, back_down = (
        lax.all_gather(again_attend, "dp", axis=0, tiled=True),
        lax.all_gather(again_out, "dp", axis=0, tiled=True),
        lax.all_gather(again_up, "dp", axis=0, tiled=True),
        lax.all_gather(again_down, "dp", axis=0, tiled=True),
    )
    cot_low = cotangent.astype(jnp.bfloat16)
    grad_down = jnp.einsum("spf,spd->fd", gelu_output, cot_low, preferred_element_type=jnp.float32)
    grad_activ = jnp.einsum("spd,fd->spf", cot_low, back_down, preferred_element_type=jnp.float32)
    gelu_pull = jax.vjp(gelu_exact, hidden_before_gelu)[1]
    hidden_low = gelu_pull(grad_activ)[0].astype(jnp.bfloat16)
    grad_up = jnp.einsum(
        "spd,spf->df", second_normed, hidden_low, preferred_element_type=jnp.float32
    )
    grad_up_shift = jnp.sum(hidden_low.astype(jnp.float32), (0, 1))
    grad_normed_two = jnp.einsum(
        "spf,df->spd", hidden_low, back_up, preferred_element_type=jnp.float32
    )
    second_pull = jax.vjp(layer_norm, middle_hidden, column_total[:, 5], column_total[:, 6])[1]
    grad_middle_norm, gain_two, shift_two = second_pull(grad_normed_two)
    grad_middle = cotangent + grad_middle_norm
    middle_low = grad_middle.astype(jnp.bfloat16)
    grad_out = jnp.einsum("spd,spe->de", mixed_low, middle_low, preferred_element_type=jnp.float32)
    grad_mixed = jnp.einsum(
        "spe,de->spd", middle_low, back_out, preferred_element_type=jnp.float32
    ).astype(jnp.bfloat16)
    grad_mixed_blk = blocked(grad_mixed, piece_rows)

    def query_block(operands):
        return query_backward(
            operands[0], operands[1], operands[2], operands[3], operands[4], query_pos, score_scale
        )

    grad_query, row_dot = lax.map(
        query_block, (query_blk, key_blk, value_blk, grad_mixed_blk, log_total)
    )
    total_rows = log_total.reshape(seq_count, HEADS, piece_rows).transpose(0, 2, 1)
    dot_rows = row_dot.reshape(seq_count, HEADS, piece_rows).transpose(0, 2, 1)
    stats_all = lax.all_gather(jnp.stack([total_rows, dot_rows], -1), "seq", axis=1, tiled=True)
    own_keys = key_rows.reshape(seq_count, piece_rows, HEADS, head_dim)
    own_values = value_rows.reshape(seq_count, piece_rows, HEADS, head_dim)
    query_piece = lax.all_gather(query_rows, "seq", axis=1, tiled=True)
    mixed_piece = lax.all_gather(grad_mixed, "seq", axis=1, tiled=True)
    count = query_piece.shape[1]
    query_heads = query_piece.reshape(seq_count, count, HEADS, head_dim)
    mixed_heads = mixed_piece.reshape(seq_count, count, HEADS, head_dim)
    total_part = stats_all[..., 0].transpose(0, 2, 1)[..., None]
    dot_part = stats_all[..., 1].transpose(0, 2, 1)[..., None]
    piece_pos = jnp.arange(count)
    scores = masked_scores(query_heads, own_keys, piece_pos, query_pos, score_scale)
    attn_probs = jnp.exp(scores - total_part)
    grad_probs = jnp.einsum(
        "bqhe,bkhe->bhqk", mixed_heads, own_values, preferred_element_type=jnp.float32
    )
    grad_scores = (attn_probs * (grad_probs - dot_part)).astype(jnp.bfloat16)
    key_term = (
        jnp.einsum("bhqk,bqhe->bkhe", grad_scores, query_heads, preferred_element_type=jnp.float32)
        * score_scale
    )
    value_term = jnp.einsum(
        "bhqk,bqhe->bkhe",
        attn_probs.astype(jnp.bfloat16),
        mixed_heads,
        preferred_element_type=jnp.float32,
    )
    grad_key = key_term.reshape(seq_count, piece_rows, model_width)
    grad_value = value_term.reshape(seq_count, piece_rows, model_width)
    query_low = grad_query.reshape(seq_count, piece_rows, model_width).astype(jnp.bfloat16)
    key_low = grad_key.astype(jnp.bfloat16)
    value_low = grad_value.astype(jnp.bfloat16)
    joined = jnp.concatenate([query_low, key_low, value_low], -1)
    grad_attend = jnp.einsum(
        "spd,spe->de", first_normed, joined, preferred_element_type=jnp.float32
    )
    grad_normed_one = jnp.einsum(
        "spe,de->spd", joined, back_attend, preferred_element_type=jnp.float32
    )
    first_pull = jax.vjp(layer_norm, inputs, column_total[:, 0], column_total[:, 1])[1]
    grad_input_norm, gain_one, shift_one = first_pull(grad_normed_one)
    grad_inputs = grad_middle + grad_input_norm
    grad_vectors = jnp.stack(
        [
            gain_one,
            shift_one,
            jnp.sum(query_low.astype(jnp.float32), (0, 1)),
            jnp.sum(value_low.astype(jnp.float32), (0, 1)),
            jnp.sum(grad_middle, (0, 1)),
            gain_two,
            shift_two,
            jnp.sum(cotangent, (0, 1)),
        ],
        axis=1,
    )
    summed_attend, summed_out, summed_up, summed_down, summed_vec, summed_bias = (
        lax.psum_scatter(grad_attend, "dp", scatter_dimension=0, tiled=True),
        lax.psum_scatter(grad_out, "dp", scatter_dimension=0, tiled=True),
        lax.psum_scatter(grad_up, "dp", scatter_dimension=0, tiled=True),
        lax.psum_scatter(grad_down, "dp", scatter_dimension=0, tiled=True),
        lax.psum_scatter(grad_vectors, "dp", scatter_dimension=0, tiled=True),
        lax.psum_scatter(grad_up_shift, "dp", scatter_dimension=0, tiled=True),
    )
    owned_attend, owned_out, owned_up, owned_down, owned_vec, owned_bias = (
        lax.psum_scatter(summed_attend, "seq", scatter_dimension=1, tiled=True),
        lax.psum_scatter(summed_out, "seq", scatter_dimension=1, tiled=True),
        lax.psum_scatter(summed_up, "seq", scatter_dimension=1, tiled=True),
        lax.psum_scatter(summed_down, "seq", scatter_dimension=1, tiled=True),
        lax.psum_scatter(summed_vec, "seq", scatter_dimension=1, tiled=True),
        lax.psum_scatter(summed_bias, "seq", scatter_dimension=0, tiled=True),
    )
    return (
        outputs,
        grad_inputs,
        owned_attend,
        owned_out,
        owned_up,
        owned_down,
        owned_vec,
        owned_bias,
    )


def solution(mesh):
    placed = (
        P("dp", "seq", None),
        P("dp", "seq"),
        P("dp", "seq"),
        P("dp", "seq"),
        P("dp", "seq"),
        P("dp", "seq"),
        P(("dp", "seq")),
        P("dp", "seq", None),
    )
    return jax.shard_map(
        body,
        mesh=mesh,
        in_specs=placed,
        out_specs=(
            P("dp", "seq", None),
            P("dp", "seq", None),
            P("dp", "seq"),
            P("dp", "seq"),
            P("dp", "seq"),
            P("dp", "seq"),
            P("dp", "seq"),
            P(("dp", "seq")),
        ),
        check_vma=False,
    )
```

profile of v0, /device:TPU:0, one launch (start us, length us, event | category | flops | bytes accessed | tf_op | source)
XLA Modules:
  0.0 1223.0 jit_solution(13279373229812182374)
XLA Ops:
  8.5 9.5 all-gather.3
  19.5 5.2 all-gather.5
  25.8 4.2 all-gather.1
  30.1 22.1 %all-gather.2 = bf16[16,68,8]{1,2,0:T(8,128)(2,1)S(1)} all-gather(bf16[1,68,8]{1,2,0:T(8,128)(2,1)S(1)} %bitcast.231), channel_id=1, replica_groups=mesh['dp'=16,'seq'=2] {'dp'}, dimensions={0}, use_global_device_ids=true | all-gather | bytes 18496 | tf_op jit(solution)/shard_map/all_gather | solution.py:83
  54.0 37.7 %all-gather.28.cloned.1.call-done = bf16[16,68,3264]{2,1,0:T(8,128)(2,1)} async-done(((bf16[1,68,3264]{2,1,0:T(8,128)(2,1)}), bf16[16,68,3264]{2,1,0:T(8,128)(2,1)}) %all-gather.28.cloned.1.call-update) | async-done | bytes 7102480 | tf_op jit(solution)/shard_map/all_gather | solution.py:79
  91.6 9.6 reshape.587
  101.2 7.3 convolution_bitcast_fusion
  108.5 2.8 copy-done.10
  112.5 4.0 fusion.26
  116.7 10.5 all_gather.67
  127.3 10.2 all-gather.8
  141.7 4.9 all-reduce
  146.8 57.6 %all-reduce.1 = bf16[4352]{0:T(1024)(128)(2,1)S(1)} all-reduce(bf16[4352]{0:T(1024)(128)(2,1)S(1)} %dynamic-update-slice.1), channel_id=1, replica_groups=mesh['dp'=16,'seq'=2] {'dp'}, use_global_device_ids=true, to_apply=%add.1 | all-reduce | flops 4352 | bytes 17408
  205.4 4.4 reshape.591
  210.2 17.0 %fusion.5 = (f32[17,512]{1,0:T(8,128)S(1)}, f32[17,512,1024]{2,1,0:T(8,128)}) fusion(pred[512,1024]{1,0:T(8,128)(4,1)S(1)} %iota_compare_fusion.1, bf16[512,17,64]{0,2,1:T(8,128)(2,1)} %bitcast.207, bf16[1024,17,64]{0,2,1:T(8,128)(2,1)} %bitcast.205), kind=kOutput, calls=%fused_computation.10 | convolution fusion | flops 1167580672 | bytes 39553024 | tf_op jit(solution)/shard_map/while/body/eval_jaxpr/bqhe,bkhe->bhqk/dot_general | solution.py:24
  227.1 15.8 %fusion.3 = f32[17,512]{1,0:T(8,128)S(1)} fusion(f32[17,512,1024]{2,1,0:T(8,128)} %get-tuple-element.93, f32[17,512]{1,0:T(8,128)S(1)} %get-tuple-element.92, pred[512,1024]{1,0:T(8,128)(4,1)S(1)} %iota_compare_fusion.1), kind=kLoop, calls=%fused_computation.8 | loop fusion | flops 35642880 | bytes 36245504 | tf_op jit(solution)/shard_map/while/body/eval_jaxpr/reduce_sum | solution.py:35
  242.9 17.1 %fusion.35 = bf16[17,64,512]{2,1,0:T(8,128)(2,1)S(1)} fusion(bf16[1024,17,64]{0,2,1:T(8,128)(2,1)} %bitcast.215, f32[17,512,1024]{2,1,0:T(8,128)} %get-tuple-element.93, f32[17,512]{1,0:T(8,128)S(1)} %fusion.3, f32[17,512]{1,0:T(8,128)S(1)} %get-tuple-element.92, pred[512,1024]{1,0:T(8,128)(4,1)S(1)} %iota_compare_fusion.1), kind=kOutput, calls=%fused_computation.74 | convolution fusion | flops 1185972224 | bytes 39587840 | tf_op jit(solution)/shard_map/while/body/eval_jaxpr/bhqk,bkhe->bqhe/dot_general | solution.py:37
  260.1 1.7 fusion.78
  263.5 30.6 %all-gather.32.cloned.1.call-done = bf16[16,68,4352]{2,1,0:T(8,128)(2,1)} async-done(((bf16[1,68,4352]{2,1,0:T(8,128)(2,1)}), bf16[16,68,4352]{2,1,0:T(8,128)(2,1)}) %all-gather.32.cloned.1.call-update) | async-done | bytes 9469968 | tf_op jit(solution)/shard_map/all_gather | solution.py:81
  294.1 10.4 reshape.593
  304.5 32.5 %multiply_convert_fusion.4 = (bf16[512,4352]{1,0:T(8,128)(2,1)}, f32[512,4352]{1,0:T(8,128)}, f32[512,4352]{1,0:T(8,128)}) fusion(f32[4352]{0:T(1024)S(1)} %convert_element_type.201, bf16[1088,4352]{1,0:T(8,128)(2,1)} %reshape.593, f32[1,512,1088]{1,2,0:T(8,128)S(1)} %copy-done.5, f32[1088]{0:T(1024)S(1)} %copy-done.42, f32[1088]{0:T(1024)S(1)} %copy-done.24, ...), kind=kOutput, calls=%fused_computation.23 | convolution fusion | flops 4998463488 | bytes 34010624 | tf_op jit(solution)/shard_map/spd,df->spf/dot_general | solution.py:128
  337.0 43.0 %all-gather.22.cloned.1.call-done = bf16[4352,1088]{1,0:T(8,128)(2,1)} async-done(((bf16[272,1088]{1,0:T(8,128)(2,1)}), bf16[4352,1088]{1,0:T(8,128)(2,1)}) %all-gather.22.cloned.1.call-update) | async-done | bytes 9469968 | tf_op jit(solution)/shard_map/all_gather | solution.py:82
  380.1 16.8 %convert_reduce_fusion = (f32[4352]{0:T(1024)}, bf16[512,4352]{1,0:T(8,128)(2,1)}) fusion(f32[512,4352]{1,0:T(8,128)} %get-tuple-element.81, bf16[4352,1088]{1,0:T(8,128)(2,1)} %all-gather.22.cloned.1.call-done, f32[1,512,1088]{1,2,0:T(8,128)} %param.15, f32[512,4352]{1,0:T(8,128)} %get-tuple-element.96, f32[4352]{0:T(1024)S(1)} %convert_element_type.201), kind=kOutput, calls=%fused_computation.21 | convolution fusion | flops 4887048192 | bytes 34015232 | tf_op jit(solution)/shard_map/spd,fd->spf/dot_general | solution.py:151
  396.8 9.1 fusion.31
  409.0 1.8 fusion.74
  410.8 2.6 convolution_convert_fusion
  414.7 12.9 %fusion.43 = f32[4352,1088]{1,0:T(8,128)} fusion(bf16[512,4352]{1,0:T(8,128)(2,1)} %get-tuple-element.80, f32[1,512,1088]{1,2,0:T(8,128)} %param.15), kind=kOutput, calls=%fused_computation.82 | convolution fusion | flops 4849172480 | bytes 25624576 | tf_op jit(solution)/shard_map/spf,spd->fd/dot_general | solution.py:150
  427.9 18.6 %fusion.79 = f32[17,1024,512]{2,1,0:T(8,128)} fusion(bf16[1024,17,64]{0,2,1:T(8,128)(2,1)} %bitcast.209, bf16[512,17,64]{0,2,1:T(8,128)(2,1)} %bitcast.208), kind=kOutput, calls=%fused_computation.140 | convolution fusion | flops 1140850688 | bytes 38993920 | tf_op jit(solution)/shard_map/bqhe,bkhe->bhqk/dot_general | solution.py:24
  446.6 30.8 %multiply_reduce_fusion = (f32[17,512]{1,0:T(8,128)S(1)}, f32[17,512,1024]{2,1,0:T(8,128)}) fusion(f32[17,512,1024]{2,1,0:T(8,128)} %get-tuple-element.93, f32[17,512]{1,0:T(8,128)S(1)} %log_add_fusion, pred[512,1024]{1,0:T(8,128)(4,1)S(1)} %iota_compare_fusion.1, bf16[512,17,64]{0,2,1:T(8,128)(2,1)S(1)} %bitcast.213, bf16[1024,17,64]{0,2,1:T(8,128)(2,1)S(1)} %bitcast.216), kind=kOutput, calls=%fused_computation.3 | convolution fusion | flops 1185406464 | bytes 75239424 | tf_op jit(solution)/shard_map/while/body/eval_jaxpr/bqhe,bkhe->bhqk/dot_general | solution.py:47
  477.5 5.6 all_gather.74
  483.1 3.9 fusion.40
  487.0 10.1 fusion.67
  497.1 26.5 %convert_reduce_fusion.2 = (f32[17,64]{1,0:T(8,128)}, bf16[17,64,512]{2,1,0:T(8,128)(2,1)}) fusion(bf16[1024,17,64]{0,2,1:T(8,128)(2,1)S(1)} %bitcast.206, f32[17,512,1024]{2,1,0:T(8,128)} %get-tuple-element.100, f32[17,512,1024]{2,1,0:T(8,128)} %get-tuple-element.93, f32[17,512]{1,0:T(8,128)S(1)} %get-tuple-element.99, f32[17,512]{1,0:T(8,128)S(1)} %log_add_fusion, ...), kind=kOutput, calls=%fused_computation.62 | convolution fusion | flops 1196555264 | bytes 75243776 | tf_op jit(solution)/shard_map/while/body/eval_jaxpr/bhqk,bkhe->bqhe/dot_general | solution.py:60
  523.6 17.5 %convert_reduce_fusion.1 = (f32[17,64]{1,0:T(8,128)}, bf16[17,64,512]{2,1,0:T(8,128)(2,1)}) fusion(bf16[1024,17,64]{0,2,1:T(8,128)(2,1)} %bitcast.232, f32[17,1024,512]{2,1,0:T(8,128)} %fusion.79, f32[17,1024]{1,0:T(8,128)S(1)} %get-tuple-element.86, pred[1024,512]{1,0:T(8,128)(4,1)} %iota_compare_fusion), kind=kOutput, calls=%fused_computation.61 | convolution fusion | flops 1178172416 | bytes 39592192 | tf_op jit(solution)/shard_map/bhqk,bqhe->bkhe/dot_general | solution.py:202
  541.1 20.7 %multiply_convert_fusion.5 = bf16[17,64,512]{2,1,0:T(8,128)(2,1)} fusion(bf16[1024,17,64]{0,2,1:T(8,128)(2,1)} %bitcast.210, f32[17,1024,512]{2,1,0:T(8,128)} %fusion.79, f32[17,1024]{1,0:T(8,128)S(1)} %get-tuple-element.85, f32[17,1024]{1,0:T(8,128)S(1)} %get-tuple-element.86, pred[1024,512]{1,0:T(8,128)(4,1)} %iota_compare_fusion, ...), kind=kOutput, calls=%fused_computation.64 | convolution fusion | flops 2336292864 | bytes 42999808 | tf_op jit(solution)/shard_map/bhqk,bqhe->bkhe/dot_general | solution.py:199
  561.9 11.3 fusion.36
  573.1 431.3 %fusion.73 = (f32[72,3264]{1,0:T(8,128)}, f32[80,1088]{1,0:T(8,128)}, f32[72,4352]{1,0:T(8,128)S(1)}) fusion(f32[1088,3264]{1,0:T(8,128)} %fusion.36, f32[1088,1088]{1,0:T(8,128)} %fusion.40, f32[1088,4352]{1,0:T(8,128)} %fusion.67), kind=kCustom, calls=%all-reduce-scatter.3 | all-reduce-scatter fusion | flops 10166274 | bytes 40421888
  1004.4 2.1 slice.68
  1006.6 33.6 %collective-permute-start = (f32[60,3264]{1,0:T(8,128)}, f32[60,3264]{1,0:T(8,128)}, u32[]{:S(2)}, u32[]{:S(2)}) collective-permute-start(f32[60,3264]{1,0:T(8,128)} %slice.68), channel_id=1, source_target_pairs={{0,2},{2,4},{4,6},{6,8},{8,10},{10,12},{12,14},{14,16},{16,18},{18... | collective-permute-start | bytes 2350088
  1040.2 4.3 collective-permute-start.1
  1044.5 2.0 collective-permute-start.2
  1048.0 2.4 collective-permute-start.3
  1051.1 6.3 collective-permute-done.3
  1057.5 6.9 concatenate.5
  1064.4 1.7 constant_dynamic-slice_fusion.1
  1066.2 2.0 copy.29
  1068.9 7.7 concatenate.4
  1076.7 2.2 constant_dynamic-slice_fusion.2
  1078.9 3.0 copy.27
  1082.0 3.0 copy.31
  1087.6 1.9 reduce_sum.205
  1090.3 10.3 collective-permute-start.4
  1100.6 14.0 %fusion.23 = f32[1,512,1088]{1,2,0:T(8,128)} fusion(f32[1,512,1088]{1,2,0:T(8,128)} %copy-done.4, bf16[512,4352]{1,0:T(8,128)(2,1)} %get-tuple-element.80, bf16[4352,1088]{1,0:T(8,128)(2,1)} %all-gather.22.cloned.1.call-done, f32[1088]{0:T(1024)S(1)} %copy-done.40), kind=kOutput, calls=%fused_computation.43 | convolution fusion | flops 4849729536 | bytes 18387200 | tf_op jit(solution)/shard_map/spf,fd->spd/dot_general | solution.py:134
  1114.5 8.7 concatenate.6
  1123.2 2.6 constant_dynamic-slice_fusion
  1125.9 9.6 fusion.30
  1135.4 1.9 reduce_sum.197
  1137.4 2.6 fusion.29
  1140.1 59.1 %all-reduce.12 = (f32[1088,8]{0,1:T(8,128)S(1)}, f32[4352]{0:T(1024)S(1)}) all-reduce(f32[1088,8]{0,1:T(8,128)S(1)} %stack.47, f32[4352]{0:T(1024)S(1)} %copy-done.33), channel_id=11, replica_groups=mesh['dp'=16,'seq'=2] {'dp'}, use_global_device_ids=true, to_apply=%region_27.28.clone | all-reduce | flops 13056 | bytes 104448
  1199.3 5.0 all-reduce.13
  1205.5 4.3 add_add_fusion.2
  1209.9 1.8 copy.30
  1211.7 2.2 copy.28
  1213.9 2.3 copy.32
  (195 shorter events, 22.0 us)
Async XLA Ops:
  7.2 12.3 %copy-start.21 = (f32[68,544]{1,0:T(8,128)S(1)}, f32[68,544]{1,0:T(8,128)}, u32[]{:S(2)}) copy-start(f32[68,544]{1,0:T(8,128)} %param.10) | copy-start | bytes 443908
  7.2 18.6 %copy-start.46 = (f32[68,4]{0,1:T(4,128)S(1)}, f32[68,4]{0,1:T(4,128)}, u32[]{:S(2)}) copy-start(f32[68,4]{0,1:T(4,128)} %param.13) | copy-start | bytes 3268
  7.2 45.0 %copy-start = (f32[1,512,1088]{1,2,0:T(8,128)S(1)}, f32[1,512,1088]{1,2,0:T(8,128)}, u32[]{:S(2)}) copy-start(f32[1,512,1088]{1,2,0:T(8,128)} %param.8) | copy-start | bytes 6684676
  7.2 84.4 %all-gather.28.cloned.1.call-start = ((), (), s32[]{:S(2)}) async-start(), calls=%async_computation.12 | async-start | bytes 8146944 | tf_op jit(solution)/shard_map/all_gather | solution.py:79
  19.4 186.0 %all-gather.30.cloned.1.call-start = ((), (), s32[]{:S(2)}) async-start(), calls=%async_computation.13 | async-start | bytes 2820096 | tf_op jit(solution)/shard_map/all_gather | solution.py:80
  25.7 184.4 %all-gather.20.cloned.1.call-start = ((), (), s32[]{:S(2)}) async-start(), calls=%async_computation.6 | async-start | bytes 3342336 | tf_op jit(solution)/shard_map/all_gather | solution.py:98
  53.1 48.1 %copy-start.22 = (f32[1088]{0:T(1024)}, f32[1088]{0:T(1024)S(1)}, u32[]{:S(2)}) copy-start(f32[1088]{0:T(1024)S(1)} %get-tuple-element.67) | copy-start | bytes 13060
  53.1 48.1 %copy-start.41 = (f32[1088]{0:T(1024)}, f32[1088]{0:T(1024)S(1)}, u32[]{:S(2)}) copy-start(f32[1088]{0:T(1024)S(1)} %get-tuple-element.66) | copy-start | bytes 13060
  53.1 48.1 %copy-start.27 = (f32[512]{0:T(512)}, f32[512]{0:T(512)S(1)}, u32[]{:S(2)}) copy-start(f32[512]{0:T(512)S(1)} %broadcast_multiply_fusion.1) | copy-start | bytes 6148
  53.9 47.3 %copy-start.29 = (f32[512]{0:T(512)}, f32[512]{0:T(512)S(1)}, u32[]{:S(2)}) copy-start(f32[512]{0:T(512)S(1)} %fusion.53) | copy-start | bytes 6148
  108.5 2.8 copy-start.10
  112.4 130.5 %all-gather.18.cloned.1.call-start = ((), (), s32[]{:S(2)}) async-start(), calls=%async_computation.5 | async-start | bytes 3342336 | tf_op jit(solution)/shard_map/all_gather | solution.py:99
  112.5 4.1 copy-start.20
  116.5 10.7 copy-start.19
  116.6 177.6 %all-gather.32.cloned.1.call-start = ((), (), s32[]{:S(2)}) async-start(), calls=%async_computation.14 | async-start | bytes 10653696 | tf_op jit(solution)/shard_map/all_gather | solution.py:81
  127.2 12.2 %copy-start.47 = (f32[136]{0:T(256)S(1)}, f32[136]{0:T(256)}, u32[]{:S(2)}) copy-start(f32[136]{0:T(256)} %param.14) | copy-start | bytes 1636
  127.2 12.3 %copy-start.44 = (u32[32]{0:T(128)S(1)}, u32[32]{0:T(128)}, u32[]{:S(2)}) copy-start(u32[32]{0:T(128)} %constant.146) | copy-start | bytes 388
  127.2 12.3 %copy-start.45 = (u32[32]{0:T(128)S(1)}, u32[32]{0:T(128)}, u32[]{:S(2)}) copy-start(u32[32]{0:T(128)} %constant.141) | copy-start | bytes 388
  127.2 252.9 %all-gather.22.cloned.1.call-start = ((), (), s32[]{:S(2)}) async-start(), calls=%async_computation.7 | async-start | bytes 10653696 | tf_op jit(solution)/shard_map/all_gather | solution.py:82
  139.3 288.6 %all-gather.24.cloned.1.call-start = ((), (), s32[]{:S(2)}) async-start(), calls=%async_computation.8 | async-start | bytes 3342336 | tf_op jit(solution)/shard_map/all_gather | solution.py:184
  209.9 313.7 %all-gather.26.cloned.1.call-start = ((), (), s32[]{:S(2)}) async-start(), calls=%async_computation.11 | async-start | bytes 3342336 | tf_op jit(solution)/shard_map/all_gather | solution.py:185
  242.9 17.2 %copy-start.14 = (bf16[1088,1088]{1,0:T(8,128)(2,1)S(1)}, bf16[1088,1088]{1,0:T(8,128)(2,1)}, u32[]{:S(2)}) copy-start(bf16[1088,1088]{1,0:T(8,128)(2,1)} %reshape.591) | copy-start | bytes 7102468
  242.9 17.2 %copy-start.43 = (f32[1088]{0:T(1024)S(1)}, f32[1088]{0:T(1024)}, u32[]{:S(2)}) copy-start(f32[1088]{0:T(1024)} %get-tuple-element.54) | copy-start | bytes 13060
  263.5 41.0 %copy-start.5 = (f32[1,512,1088]{1,2,0:T(8,128)S(1)}, f32[1,512,1088]{1,2,0:T(8,128)}, u32[]{:S(2)}) copy-start(f32[1,512,1088]{1,2,0:T(8,128)} %copy-done.4) | copy-start | bytes 6684676
  263.5 41.0 %copy-start.24 = (f32[1088]{0:T(1024)S(1)}, f32[1088]{0:T(1024)}, u32[]{:S(2)}) copy-start(f32[1088]{0:T(1024)} %get-tuple-element.53) | copy-start | bytes 13060
  263.5 41.0 %copy-start.42 = (f32[1088]{0:T(1024)S(1)}, f32[1088]{0:T(1024)}, u32[]{:S(2)}) copy-start(f32[1088]{0:T(1024)} %get-tuple-element.52) | copy-start | bytes 13060
  405.9 4.9 copy-start.8
  405.9 2.4 copy-start.6
  405.9 3.1 copy-start.16
  409.0 1.8 copy-start.15
  410.8 72.3 %copy-start.3 = (f32[1,512,1088]{1,2,0:T(8,128)}, f32[1,512,1088]{1,2,0:T(8,128)S(1)}, u32[]{:S(2)}) copy-start(f32[1,512,1088]{1,2,0:T(8,128)S(1)} %get-tuple-element.79) | copy-start | bytes 6684676
  410.8 2.7 copy-start.35
  413.5 668.5 %reduce-scatter.21.cloned.1.call-start = ((), (), s32[]{:S(2)}) async-start(), calls=%async_computation.10 | async-start | bytes 21307392 | tf_op jit(solution)/shard_map/reduce_scatter | solution.py:240
  427.6 782.2 %reduce-scatter.25.cloned.1.call-start = ((), (), s32[]{:S(2)}) async-start(), calls=%async_computation.16 | async-start | bytes 835584
  427.9 18.7 %copy-start.9 = (bf16[512,1088]{0,1:T(8,128)(2,1)S(1)}, bf16[512,1088]{0,1:T(8,128)(2,1)}, u32[]{:S(2)}) copy-start(bf16[512,1088]{0,1:T(8,128)(2,1)} %convolution_convert_fusion) | copy-start | bytes 3342340
  427.9 18.7 %copy-start.12 = (bf16[1,1024,1088]{1,2,0:T(8,128)(2,1)S(1)}, bf16[1,1024,1088]{1,2,0:T(8,128)(2,1)}, u32[]{:S(2)}) copy-start(bf16[1,1024,1088]{1,2,0:T(8,128)(2,1)} %all-gather.18.cloned.1.call-done) | copy-start | bytes 6684676
  427.9 59.1 %slice-start = ((s8[4456448]{0:T(1024)(128)(4,1)}), s8[4194304]{0:T(1024)(128)(4,1)S(1)}, s32[]{:S(2)}) async-start(s8[4456448]{0:T(1024)(128)(4,1)} %bitcast.238), calls=%async_computation.18 | async-start | bytes 8388608
  446.6 36.5 %copy-start.18 = (bf16[17,64,512]{2,1,0:T(8,128)(2,1)S(1)}, bf16[17,64,512]{2,1,0:T(8,128)(2,1)}, u32[]{:S(2)}) copy-start(bf16[17,64,512]{2,1,0:T(8,128)(2,1)} %copy-done.17) | copy-start | bytes 3342340
  446.6 40.4 %slice-start.1 = ((s8[4456448]{0:T(1024)(128)(4,1)}), s8[262144]{0:T(1024)(128)(4,1)S(1)}, s32[]{:S(2)}) async-start(s8[4456448]{0:T(1024)(128)(4,1)} %bitcast.238), calls=%async_computation.19 | async-start | bytes 524288
  483.1 3.9 copy-start.7
  487.0 10.1 copy-start.2
  523.6 17.5 %copy-start.11 = (bf16[1,512,1088]{1,2,0:T(8,128)(2,1)S(1)}, bf16[1,512,1088]{1,2,0:T(8,128)(2,1)}, u32[]{:S(2)}) copy-start(bf16[1,512,1088]{1,2,0:T(8,128)(2,1)} %get-tuple-element.83) | copy-start | bytes 3342340
  541.1 20.7 %copy-start.1 = (f32[1,512,1088]{1,2,0:T(8,128)S(1)}, f32[1,512,1088]{1,2,0:T(8,128)}, u32[]{:S(2)}) copy-start(f32[1,512,1088]{1,2,0:T(8,128)} %param.8) | copy-start | bytes 6684676
  541.1 20.8 %copy-start.23 = (f32[1088]{0:T(1024)S(1)}, f32[1088]{0:T(1024)}, u32[]{:S(2)}) copy-start(f32[1088]{0:T(1024)} %copy-done.22) | copy-start | bytes 13060
  541.1 20.8 %copy-start.28 = (f32[512]{0:T(512)S(1)}, f32[512]{0:T(512)}, u32[]{:S(2)}) copy-start(f32[512]{0:T(512)} %copy-done.27) | copy-start | bytes 6148
  541.1 20.8 %copy-start.30 = (f32[512]{0:T(512)S(1)}, f32[512]{0:T(512)}, u32[]{:S(2)}) copy-start(f32[512]{0:T(512)} %copy-done.29) | copy-start | bytes 6148
  1006.6 62.4 %collective-permute-start = (f32[60,3264]{1,0:T(8,128)}, f32[60,3264]{1,0:T(8,128)}, u32[]{:S(2)}, u32[]{:S(2)}) collective-permute-start(f32[60,3264]{1,0:T(8,128)} %slice.68), channel_id=1, source_target_pairs={{0,2},{2,4},{4,6},{6,8},{8,10},{10,12},{12,14},{14,16},{16,18},{18... | collective-permute-start | bytes 2350088
  1040.2 17.3 %collective-permute-start.1 = (f32[80,1088]{1,0:T(8,128)}, f32[80,1088]{1,0:T(8,128)}, u32[]{:S(2)}, u32[]{:S(2)}) collective-permute-start(f32[80,1088]{1,0:T(8,128)} %get-tuple-element.76), channel_id=1, source_target_pairs={{0,2},{2,4},{4,6},{6,8},{8,10},{10,12},{12,14},{14,16},{16,18},{18... | collective-permute-start | bytes 1044488
  1044.5 13.0 %collective-permute-start.2 = (f32[80,1088]{1,0:T(8,128)}, f32[80,1088]{1,0:T(8,128)}, u32[]{:S(2)}, u32[]{:S(2)}) collective-permute-start(f32[80,1088]{1,0:T(8,128)} %get-tuple-element.76), channel_id=1, source_target_pairs={{0,4},{2,6},{4,8},{6,10},{8,12},{10,14},{12,16},{14,18},{16,20},{1... | collective-permute-start | bytes 1044488
  1048.0 9.4 collective-permute-start.3
  1068.2 143.5 %reduce-scatter.23.cloned.1.call-start = ((), (), s32[]{:S(2)}) async-start(), calls=%async_computation.15 | async-start | bytes 2506752
  1081.9 132.0 %reduce-scatter.27.cloned.1.call-start = ((), (), s32[]{:S(2)}) async-start(), calls=%async_computation.17 | async-start | bytes 2506752
  1085.0 4.5 copy-start.25
  1085.0 5.2 copy-start.32
  1085.0 5.2 copy-start.31
  1085.0 5.2 copy-start.26
  1085.0 15.6 %copy-start.40 = (f32[1088]{0:T(1024)S(1)}, f32[1088]{0:T(1024)}, u32[]{:S(2)}) copy-start(f32[1088]{0:T(1024)} %get-tuple-element.51) | copy-start | bytes 13060
  1085.0 131.2 %reduce-scatter.19.cloned.1.call-start = ((), (), s32[]{:S(2)}) async-start(), calls=%async_computation.9 | async-start | bytes 1880064 | tf_op jit(solution)/shard_map/reduce_scatter | solution.py:247
  1090.3 24.2 %collective-permute-start.4 = (f32[60,4352]{1,0:T(8,128)S(1)}, f32[60,4352]{1,0:T(8,128)}, u32[]{:S(2)}, u32[]{:S(2)}) collective-permute-start(f32[60,4352]{1,0:T(8,128)S(1)} %slice.70), channel_id=1, source_target_pairs={{0,2},{2,4},{4,6},{6,8},{8,10},{10,12},{12,14},{14,16},{16,18},{18... | collective-permute-start | bytes 3133448
  1123.2 2.6 copy-start.13
  1125.8 11.5 copy-start.38
  1137.3 2.6 copy-start.39
  1137.3 2.7 copy-start.36
  1137.4 2.8 copy-start.33
  (4 other events, 4.2 us)
Sparse Core Ops, SparseCore 0:
  19.6 72.0 all-gather.27
  94.3 41.6 all-gather.29
  137.6 33.2 all-gather.19
  172.3 34.6 all-gather.17
  209.0 85.1 all-gather.31
  296.7 83.2 all-gather.21
  381.6 32.7 all-gather.23
  416.0 34.5 all-gather.25
  454.8 288.0 reduce-scatter.20
  1068.3 22.0 reduce-scatter.24
  1092.8 27.1 reduce-scatter.22
  1122.2 27.1 reduce-scatter.26
  1152.3 22.5 reduce-scatter.18
where the time goes:
time: 1230 us; the launch traced here: 1220 us
  blocking collectives  625 us (51%)
  matrix products  280 us (23%)
  waiting for transfers between devices  118 us (10%)
  local copies, waits for them, and re-layouts  88.8 us (7%)
  starting transfers between devices  53.5 us (4%)
  other arithmetic  37.5 us (3%)
  between operations  20.1 us (2%)
    unnamed x5, blocking collectives  558 us
    unnamed x130, local copies, waits for them, and re-layouts  85 us
    unnamed x8, starting transfers between devices  52.9 us
    all_gather x1, waiting for transfers between devices, body(): lax.all_gather(seq_down, 'dp', axis=0, tiled=True)  43 us
    all_gather x1, waiting for transfers between devices, body(): lax.all_gather(seq_attend, 'dp', axis=0, tiled=True)  37.7 us
    dot_general x2, matrix products, masked_scores(): jnp.einsum('bqhe,bkhe->bhqk', query_rows, key_rows, preferred_element_typ...  35.6 us
    dot_general x1, matrix products, body(): jnp.einsum('spd,df->spf', second_normed, full_up, preferred_element_type=...  32.5 us
    dot_general x1, matrix products, score_grads(): jnp.einsum('bqhe,bkhe->bhqk', grad_mixed, value_rows, preferred_element_t...  30.8 us
  transfers between devices with their start and end apart: 18, of which 4 were waited for; matrix products, arithmetic and copies ran while one was open for 68% of the time, Pallas kernels for 0%

commit v1 on v0

v1 whole, which is shorter than its diff:
```python
import functools
import math

import jax
import jax.numpy as jnp
from jax import lax
from jax.experimental import pallas as pl
from jax.experimental.pallas import tpu as pltpu
from jax.sharding import PartitionSpec as P

HEADS = 17
HEAD_DIM = 64
BF = jnp.bfloat16
F32 = jnp.float32


def dot(left, right, dims):
    return lax.dot_general(left, right, (dims, ((), ())), preferred_element_type=F32)


def norm_parts(values):
    center = values - jnp.mean(values, -1, keepdims=True)
    spread = jnp.mean(center * center, -1, keepdims=True)
    inv = lax.rsqrt(spread + 1e-05)
    return center * inv, inv


def norm_grad(normed, inv, gain, upstream):
    scaled = gain * upstream
    first = jnp.mean(scaled, -1, keepdims=True)
    second = jnp.mean(scaled * normed, -1, keepdims=True)
    return (scaled - first - normed * second) * inv


def half_mask(rows, head):
    lane = lax.broadcasted_iota(jnp.int32, (rows, 128), 1)
    return (lane < HEAD_DIM) if head == 0 else (lane >= HEAD_DIM)


def causal(scores, offset):
    rows, cols = scores.shape
    query = lax.broadcasted_iota(jnp.int32, (rows, cols), 0) + offset
    keyp = lax.broadcasted_iota(jnp.int32, (rows, cols), 1)
    return jnp.where(keyp <= query, scores, -1e30)


def attend_kernel(q_ref, k_ref, v_ref, o_ref, l_ref):
    rows = q_ref.shape[1]
    offset = lax.axis_index("seq") * rows
    q, k, v = q_ref[0], k_ref[0], v_ref[0]
    zero = jnp.zeros_like(q)
    outs, logs = [], []
    for head in range(2):
        mask = half_mask(rows, head)
        scores = dot(jnp.where(mask, q, zero), k, ((1,), (1,))) * (1.0 / math.sqrt(HEAD_DIM))
        scores = causal(scores, offset)
        top = jnp.max(scores, -1, keepdims=True)
        raised = jnp.exp(scores - top)
        total = jnp.sum(raised, -1, keepdims=True)
        probs = (raised * (1.0 / total)).astype(BF)
        outs.append(dot(probs, v, ((1,), (0,))))
        logs.append(top + jnp.log(total))
    mask = half_mask(rows, 0)
    o_ref[0] = jnp.where(mask, outs[0], outs[1]).astype(BF)
    l_ref[0] = jnp.where(mask, logs[0], logs[1])


def attend_back_kernel(q_ref, k_ref, v_ref, g_ref, l_ref, dq_ref, dk_ref, dv_ref):
    rows = q_ref.shape[1]
    offset = lax.axis_index("seq") * rows
    q, k, v, g = q_ref[0], k_ref[0], v_ref[0], g_ref[0]
    zero = jnp.zeros_like(q)
    scale = 1.0 / math.sqrt(HEAD_DIM)
    dqs = []
    dk = dv = None
    for head in range(2):
        mask = half_mask(rows, head)
        qm, gm = jnp.where(mask, q, zero), jnp.where(mask, g, zero)
        scores = causal(dot(qm, k, ((1,), (1,))) * scale, offset)
        probs = jnp.exp(scores - l_ref[0, :, head * HEAD_DIM : head * HEAD_DIM + 1])
        grad_probs = dot(gm, v, ((1,), (1,)))
        row_dot = jnp.sum(probs * grad_probs, -1, keepdims=True)
        grad_scores = (probs * (grad_probs - row_dot)).astype(BF)
        low = probs.astype(BF)
        dqs.append(dot(grad_scores, k, ((1,), (0,))) * scale)
        dk_part = dot(grad_scores, qm, ((0,), (0,)))
        dv_part = dot(low, gm, ((0,), (0,)))
        dk = dk_part if dk is None else dk + dk_part
        dv = dv_part if dv is None else dv + dv_part
    dq_ref[0] = jnp.where(half_mask(rows, 0), dqs[0], dqs[1]).astype(BF)
    dk_ref[0] = dk * scale
    dv_ref[0] = dv


def attend(q, k, v):
    seqs, rows, width = q.shape
    length = k.shape[1]
    pairs = width // 128
    small = pl.BlockSpec((1, rows, 128), lambda s, h: (s, 0, h))
    large = pl.BlockSpec((1, length, 128), lambda s, h: (s, 0, h))
    work = seqs * pairs * 2 * rows * length
    return pl.pallas_call(
        attend_kernel,
        grid=(seqs, pairs),
        in_specs=[small, large, large],
        out_specs=[small, small],
        out_shape=[
            jax.ShapeDtypeStruct(q.shape, BF),
            jax.ShapeDtypeStruct(q.shape, F32),
        ],
        compiler_params=pltpu.CompilerParams(vmem_limit_bytes=48 * 2**20),
        cost_estimate=pl.CostEstimate(
            flops=work * 1024, bytes_accessed=8 * q.size + 4 * k.size, transcendentals=work
        ),
    )(q, k, v)


def attend_back(q, k, v, g, logs):
    seqs, rows, width = q.shape
    length = k.shape[1]
    pairs = width // 128
    small = pl.BlockSpec((1, rows, 128), lambda s, h: (s, 0, h))
    large = pl.BlockSpec((1, length, 128), lambda s, h: (s, 0, h))
    work = seqs * pairs * 2 * rows * length
    return pl.pallas_call(
        attend_back_kernel,
        grid=(seqs, pairs),
        in_specs=[small, large, large, small, small],
        out_specs=[small, large, large],
        out_shape=[
            jax.ShapeDtypeStruct(q.shape, BF),
            jax.ShapeDtypeStruct(k.shape, F32),
            jax.ShapeDtypeStruct(k.shape, F32),
        ],
        compiler_params=pltpu.CompilerParams(vmem_limit_bytes=52 * 2**20),
        cost_estimate=pl.CostEstimate(
            flops=work * 2560, bytes_accessed=10 * q.size + 12 * k.size, transcendentals=work
        ),
    )(q, k, v, g, logs)


def exchange(value, axis, size, stride):
    return lax.ppermute(value, axis, [(i, i ^ stride) for i in range(size)])


def scatter_sum(left_blocks, right_pieces, dp, seq):
    tokens, _, rows = left_blocks.shape
    cols = right_pieces.shape[-1]
    me, piece = lax.axis_index("dp"), lax.axis_index("seq")
    pairs = left_blocks.reshape(tokens, dp // 2, 2, rows)
    bit = me % 2

    def pick(which):
        return lax.dynamic_index_in_dim(pairs, which, 2, False).reshape(tokens, dp // 2 * rows)

    def piece_at(which):
        return lax.dynamic_index_in_dim(right_pieces, which, 1, False)

    away, near = pick(1 - bit), pick(bit)
    held = []
    for step in range(seq - 1, -1, -1):
        right = piece_at(piece ^ step)
        sent = dot(away, right, ((0,), (0,))).astype(BF)
        got = exchange(sent, "dp", dp, 1)
        held.append(dot(near, right, ((0,), (0,))) + got.astype(F32))
    held = held[::-1]
    half = seq // 2
    while half >= 1:
        kept = []
        for step in range(half):
            got = exchange(held[step + half].astype(BF), "seq", seq, half)
            kept.append(held[step] + got.astype(F32))
        held, half = kept, half // 2
    total = held[0].reshape(dp // 2, rows, cols)
    stride = 2
    while stride < dp:
        bit = (me // stride) % 2
        split = total.reshape(-1, 2, rows, cols)
        sent = lax.dynamic_index_in_dim(split, 1 - bit, 1, False).astype(BF)
        own = lax.dynamic_index_in_dim(split, bit, 1, False)
        total = own + exchange(sent, "dp", dp, stride).astype(F32)
        stride *= 2
    return total.reshape(rows, cols)


def pad_rows(block):
    extra = -block.shape[0] % 8
    return jnp.pad(block, ((0, extra), (0, 0))) if extra else block


def body(dp, seq, inputs, attend_weight, out_weight, up_weight, down_weight, vectors, up_bias, cotangent):
    seqs, rows, width = inputs.shape
    tokens = seqs * rows
    block = attend_weight.shape[0]
    tall = block + (-block % 8)
    piece = lax.axis_index("seq")
    x = inputs.reshape(tokens, width)
    cot = cotangent.reshape(tokens, width)

    few = jnp.concatenate([vectors.astype(BF).reshape(-1), up_bias.astype(BF)])
    filled = jnp.pad(few, (0, -few.size % 1024)).reshape(-1, 128)
    few = lax.all_gather(filled, ("dp", "seq"), axis=0, tiled=True).reshape(dp * seq, -1)
    vec = few[:, : vectors.size].reshape(dp, seq, block, vectors.shape[1])
    vec = vec.transpose(1, 3, 0, 2).reshape(8, width).astype(F32)
    bias = few[:, vectors.size : vectors.size + up_bias.size].reshape(-1).astype(F32)

    def columns(weight):
        pieces = lax.all_gather(pad_rows(weight.astype(BF)), "seq", axis=0)
        return jnp.concatenate([pieces[i] for i in range(seq)], -1)

    def whole(part):
        return lax.all_gather(part, "dp", axis=0, tiled=True)

    attend_full = whole(columns(attend_weight))
    out_cols, up_cols = columns(out_weight), columns(up_weight)
    joint = whole(jnp.concatenate([out_cols, up_cols], -1))
    out_full, up_full = joint[:, :width], joint[:, width:]
    down_full = whole(columns(down_weight))

    def spread(values):
        blocks = values.reshape(values.shape[0], dp, block)
        return jnp.pad(blocks, ((0, 0), (0, 0), (0, tall - block)))

    def wide(values):
        return spread(values).reshape(values.shape[0], dp * tall)

    def narrow(values):
        return values.reshape(values.shape[0], dp, tall)[:, :, :block].reshape(-1, width)

    normed_one, inv_one = norm_parts(x)
    first = (normed_one * vec[0] + vec[1]).astype(BF)
    every = lax.all_gather(first.reshape(seqs, rows, width), "seq", axis=1, tiled=True)
    length = every.shape[1]
    first_wide = wide(first)
    every_wide = wide(every.reshape(seqs * length, width))
    lanes = -width % 128

    def padded(values, count):
        return jnp.pad(values.reshape(seqs, count, width), ((0, 0), (0, 0), (0, lanes)))

    query = padded((dot(first_wide, attend_full[:, :width], ((1,), (0,))) + vec[2]).astype(BF), rows)
    both = dot(every_wide, attend_full[:, width:], ((1,), (0,)))
    keys = padded(both[:, :width].astype(BF), length)
    vals = padded((both[:, width:] + vec[3]).astype(BF), length)
    mixed, logs = attend(query, keys, vals)
    mixed_low = mixed[..., :width].reshape(tokens, width)
    cot_low = cot.astype(BF)

    out_rows = narrow(out_full.T)
    middle = x + dot(mixed_low, out_full.reshape(dp, tall, width)[:, :block].reshape(width, width), ((1,), (0,))) + vec[4]
    normed_two, inv_two = norm_parts(middle)
    second = (normed_two * vec[5] + vec[6]).astype(BF)
    hidden = dot(wide(second), up_full, ((1,), (0,))) + bias
    cdf = 0.5 * (1.0 + lax.erf(hidden * math.sqrt(0.5)))
    gelu = (hidden * cdf).astype(BF)
    slope = cdf + hidden * (jnp.exp(-0.5 * hidden * hidden) * (1.0 / math.sqrt(2 * math.pi)))
    outputs = middle + dot(gelu, down_full, ((1,), (0,))) + vec[7]

    ff_block = down_weight.shape[0]
    own_down = scatter_sum(
        gelu.reshape(tokens, dp, ff_block), cot_low.reshape(tokens, seq, -1), dp, seq
    )
    hidden_low = (slope * dot(cot_low, down_full, ((1,), (1,)))).astype(BF)
    grad_bias = jnp.sum(hidden_low.astype(F32), 0)
    own_up = scatter_sum(spread(second), hidden_low.reshape(tokens, seq, -1), dp, seq)
    grad_second = narrow(dot(hidden_low, up_full, ((1,), (1,))))
    grad_middle = cot + norm_grad(normed_two, inv_two, vec[5], grad_second)
    middle_low = grad_middle.astype(BF)
    grad_mixed = dot(middle_low, out_rows, ((1,), (0,))).astype(BF)
    own_out = scatter_sum(spread(mixed_low), middle_low.reshape(tokens, seq, -1), dp, seq)

    dq, dk, dv = attend_back(query, keys, vals, padded(grad_mixed, rows), logs)

    def piece_sum(part):
        pieces = part.reshape(seqs, seq, rows, part.shape[-1])
        total = lax.dynamic_index_in_dim(pieces, piece, 1, False)
        for step in range(1, seq):
            sent = lax.dynamic_index_in_dim(pieces, jnp.maximum(piece - step, 0), 1, False)
            got = lax.ppermute(sent[..., :width].astype(BF), "seq", [(i, i - step) for i in range(step, seq)])
            total = total + jnp.pad(got.astype(F32), ((0, 0), (0, 0), (0, lanes)))
        return total[..., :width].astype(BF).reshape(tokens, width)

    query_low = dq[..., :width].reshape(tokens, width)
    key_low, value_low = piece_sum(dk), piece_sum(dv)
    joined = jnp.concatenate([query_low, key_low, value_low], -1)
    own_attend = scatter_sum(spread(first), joined.reshape(tokens, seq, -1), dp, seq)
    grad_first = narrow(dot(joined, attend_full, ((1,), (1,))))
    grad_inputs = grad_middle + norm_grad(normed_one, inv_one, vec[0], grad_first)
    grad_vec = jnp.stack(
        [
            jnp.sum(grad_first * normed_one, 0),
            jnp.sum(grad_first, 0),
            jnp.sum(query_low.astype(F32), 0),
            jnp.sum(value_low.astype(F32), 0),
            jnp.sum(grad_middle, 0),
            jnp.sum(grad_second * normed_two, 0),
            jnp.sum(grad_second, 0),
            jnp.sum(cot, 0),
        ]
    )
    grad_vec = grad_vec.reshape(seq, -1, dp, block).transpose(2, 0, 3, 1).reshape(dp * seq, -1)
    small = jnp.concatenate([grad_vec, grad_bias.reshape(dp * seq, -1)], -1)
    small = lax.psum_scatter(small, ("dp", "seq"), scatter_dimension=0, tiled=True)[0]
    return (
        outputs.reshape(inputs.shape),
        grad_inputs.reshape(inputs.shape),
        own_attend[:block],
        own_out[:block],
        own_up[:block],
        own_down,
        small[: vectors.size].reshape(vectors.shape),
        small[vectors.size :],
    )


def solution(mesh):
    rows, tokens = P("dp", "seq"), P("dp", "seq", None)
    flat = P(("dp", "seq"))
    return jax.shard_map(
        functools.partial(body, mesh.shape["dp"], mesh.shape["seq"]),
        mesh=mesh,
        in_specs=(tokens, rows, rows, rows, rows, rows, flat, tokens),
        out_specs=(tokens, tokens, rows, rows, rows, rows, rows, flat),
        check_vma=False,
    )
```

time: 1230 us -> 932 us (0.76)
  blocking collectives: 625 us -> 198 us
  waiting for transfers between devices: 118 us -> 307 us
  matrix products: 280 us -> 130 us
  Pallas kernels: 0 us -> 63.4 us
  local copies, waits for them, and re-layouts: 88.8 us -> 132 us
  starting transfers between devices: 53.5 us -> 27.4 us
  other arithmetic: 37.5 us -> 52.8 us
    unnamed x5 -> x1, blocking collectives: 558 us -> 85.4 us
    dot_general x19 -> x25, matrix products: 280 us -> 130 us  [dot(): lax.dot_general(left, right, (dims, ((), ())), preferred_element_type=F32)]
    ppermute x0 -> x26, waiting for transfers between devices: none -> 144 us  [the longest x24 134 us: exchange(): return lax.ppermute(value, axis, [(i, i ^ stride) for i in range(size)])]
    unnamed x130 -> x145, local copies, waits for them, and re-layouts: 85 us -> 14.7 us
    pallas_call x0 -> x2, Pallas kernels: none -> 63.4 us  [the longest x1 37 us: attend_back(): pl.pallas_call(attend_back_kernel, grid=(seqs, pairs), in_specs=[small, l...]
    unnamed x8 -> x0, starting transfers between devices: 52.9 us -> none
    all_gather x8 -> x4, waiting for transfers between devices: 111 us -> 163 us  [the longest x3 163 us: whole(): return lax.all_gather(part, 'dp', axis=0, tiled=True)]
    all_gather x7 -> x5, blocking collectives: 67.2 us -> 113 us  [the longest x1 70 us: body(): lax.all_gather(filled, ('dp', 'seq'), axis=0, tiled=True)]
  transfers between devices with their start and end apart: 18 -> 30, of which waited for: 4 -> 11; matrix products, arithmetic and copies ran while one was open for 68% -> 25% of each run, Pallas kernels for 0% -> 3%
where the time goes in v1:
time: 932 us; the launch traced here: 926 us
  waiting for transfers between devices  307 us (33%)
  blocking collectives  198 us (21%)
  local copies, waits for them, and re-layouts  132 us (14%)
  matrix products  130 us (14%)
  Pallas kernels  63.4 us (7%)
  other arithmetic  52.8 us (6%)
  starting transfers between devices  27.4 us (3%)
  between operations  15.1 us (2%)
    all_gather x3, waiting for transfers between devices, whole(): return lax.all_gather(part, 'dp', axis=0, tiled=True)  163 us
    ppermute x24, waiting for transfers between devices, exchange(): return lax.ppermute(value, axis, [(i, i ^ stride) for i in range(size)])  134 us
    dot_general x25, matrix products, dot(): lax.dot_general(left, right, (dims, ((), ())), preferred_element_type=F32)  130 us
    unnamed x1, blocking collectives  85.4 us
    all_gather x1, blocking collectives, body(): lax.all_gather(filled, ('dp', 'seq'), axis=0, tiled=True)  70 us
    all_gather x4, blocking collectives, columns(): pieces = lax.all_gather(pad_rows(weight.astype(BF)), 'seq', axis=0)  42.7 us
    pallas_call x1, Pallas kernels, attend_back(): pl.pallas_call(attend_back_kernel, grid=(seqs, pairs), in_specs=[small, l...  37 us
    pallas_call x1, Pallas kernels, attend(): pl.pallas_call(attend_kernel, grid=(seqs, pairs), in_specs=[small, large,...  26.3 us
  transfers between devices with their start and end apart: 30, of which 11 were waited for; matrix products, arithmetic and copies ran while one was open for 25% of the time, Pallas kernels for 3%

profile of v1, /device:TPU:0, one launch (start us, length us, event | category | flops | bytes accessed | tf_op | source)
XLA Modules:
  0.0 926.0 jit_solution(2870871617710672916)
XLA Ops:
  9.1 70.0 %all_gather.39 = bf16[256,128]{1,0:T(8,128)(2,1)S(1)} all-gather(bf16[8,128]{1,0:T(8,128)(2,1)S(1)} %fusion.94), channel_id=1, replica_groups=mesh['dp'=16,'seq'=2] {'dp','seq'}, dimensions={0}, use_global_device_ids=true | all-gather | bytes 67584 | tf_op jit(solution)/shard_map/all_gather | solution.py:202
  83.5 8.4 all-gather
  93.0 8.2 all-gather.1
  101.2 15.6 %all-gather.2 = bf16[144,2176]{1,0:T(8,128)(2,1)S(1)} all-gather(bf16[72,2176]{1,0:T(8,128)(2,1)S(1)} %pad.67), channel_id=4, replica_groups=mesh['dp'=16,'seq'=2] {'seq'}, dimensions={0}, use_global_device_ids=true | all-gather | bytes 940032 | tf_op jit(solution)/shard_map/all_gather | solution.py:208
  119.8 10.6 %all-gather.3 = bf16[544,544]{1,0:T(8,128)(2,1)S(1)} all-gather(bf16[272,544]{1,0:T(8,128)(2,1)S(1)} %convert_element_type.311), channel_id=5, replica_groups=mesh['dp'=16,'seq'=2] {'seq'}, dimensions={0}, use_global_device_ids=true | all-gather | bytes 887808 | tf_op jit(solution)/shard_map/all_gather | solution.py:208
  140.3 2.7 reshape_reshape.21
  144.9 56.6 %all-gather.9.cloned.1.call-done = bf16[1152,3264]{1,0:T(8,128)(2,1)} async-done(((bf16[72,3264]{1,0:T(8,128)(2,1)}), bf16[1152,3264]{1,0:T(8,128)(2,1)}) %all-gather.9.cloned.1.call-update) | async-done | bytes 7520272 | tf_op jit(solution)/shard_map/all_gather | solution.py:212
  201.5 3.6 fusion.21
  207.3 9.4 %fusion.13 = f32[1024,2176]{1,0:T(8,128)S(1)} fusion(bf16[1024,1152]{0,1:T(8,128)(2,1)S(1)} %bitcast.300, bf16[1152,3264]{1,0:T(8,128)(2,1)} %all-gather.9.cloned.1.call-done), kind=kOutput, calls=%fused_computation.15 | convolution fusion | flops 5133828096 | bytes 16285696 | tf_op jit(solution)/shard_map/dot_general | solution.py:18
  221.6 26.3 %shard_map.143 = (bf16[1,512,1152]{2,1,0:T(8,128)(2,1)S(1)}, f32[1,512,1152]{2,1,0:T(8,128)S(1)}) custom-call(bf16[1,512,1152]{2,1,0:T(8,128)(2,1)S(1)} %pad.62.q_ref, bf16[1,1024,1152]{2,1,0:T(8,128)(2,1)} %pad.64.k_ref, bf16[1,1024,1152]{2,1,0:T(8,128)(2,1)} %pad.65.v_ref), custom_call_target="tpu_custom_call" | custom-call | flops 9663676416 | bytes 9437184 | tf_op jit(solution)/shard_map/pallas_call | solution.py:102
  253.1 50.9 %all-gather.13.cloned.1.call-done = bf16[1152,5440]{1,0:T(8,128)(2,1)} async-done(((bf16[72,5440]{1,0:T(8,128)(2,1)}), bf16[1152,5440]{1,0:T(8,128)(2,1)}) %all-gather.13.cloned.1.call-update) | async-done | bytes 12533776 | tf_op jit(solution)/shard_map/all_gather | solution.py:212
  304.1 3.5 slice.203
  307.6 4.5 reshape.390
  312.1 3.6 fusion.104
  321.0 13.4 %multiply_convert_fusion = (bf16[512,4352]{1,0:T(8,128)(2,1)}, f32[512,4352]{1,0:T(8,128)}) fusion(f32[4352]{0:T(1024)S(1)} %copy-done.57, bf16[512,1152]{0,1:T(8,128)(2,1)S(1)} %bitcast.270, bf16[1152,5440]{1,0:T(8,128)(2,1)} %all-gather.13.cloned.1.call-done), kind=kOutput, calls=%fused_computation.8 | convolution fusion | flops 5147197440 | bytes 24593408 | tf_op jit(solution)/shard_map/dot_general | solution.py:18
  334.4 55.5 %all-gather.15.cloned.1.call-done = bf16[4352,1088]{1,0:T(8,128)(2,1)} async-done(((bf16[272,1088]{1,0:T(8,128)(2,1)}), bf16[4352,1088]{1,0:T(8,128)(2,1)}) %all-gather.15.cloned.1.call-update) | async-done | bytes 9469968 | tf_op jit(solution)/shard_map/all_gather | solution.py:212
  389.9 14.1 %convert_reduce_fusion = (f32[4352]{0:T(1024)S(1)}, bf16[512,4352]{1,0:T(8,128)(2,1)S(1)}) fusion(bf16[4352,1088]{1,0:T(8,128)(2,1)} %all-gather.15.cloned.1.call-done, f32[512,4352]{1,0:T(8,128)} %get-tuple-element.87, f32[1,512,1088]{1,2,0:T(8,128)} %param.15), kind=kOutput, calls=%fused_computation.7 | convolution fusion | flops 4875350016 | bytes 25084928 | tf_op jit(solution)/shard_map/dot_general | solution.py:18
  404.1 9.7 %fusion.6 = f32[512,1152]{0,1:T(8,128)S(1)} fusion(bf16[512,4352]{1,0:T(8,128)(2,1)S(1)} %get-tuple-element.89, bf16[1152,5440]{1,0:T(8,128)(2,1)} %all-gather.13.cloned.1.call-done), kind=kOutput, calls=%fused_computation.10 | convolution fusion | flops 5133828096 | bytes 16842752 | tf_op jit(solution)/shard_map/dot_general | solution.py:18
  415.4 2.7 reshape.396
  418.2 3.2 multiply_reduce_fusion.3
  426.0 5.0 reshape.398
  431.0 3.6 fusion.20
  435.7 37.0 %shard_map.144 = (bf16[1,512,1152]{2,1,0:T(8,128)(2,1)S(1)}, f32[1,1024,1152]{2,1,0:T(8,128)}, f32[1,1024,1152]{2,1,0:T(8,128)}) custom-call(bf16[1,512,1152]{2,1,0:T(8,128)(2,1)} %copy-done, bf16[1,1024,1152]{2,1,0:T(8,128)(2,1)} %pad.64.k_ref, bf16[1,1024,1152]{2,1,0:T(8,128)(2,1)} %pad.65.v_ref, bf16[1,512,1152]{2,1,0:T(8,128)(2,1)} %pad.69.g_ref, ...), custom_call_target="tpu_custom_call" | custom-call | flops 24159191040 | bytes 20054016 | tf_op jit(solution)/shard_map/pallas_call | solution.py:125
  472.7 2.8 constant_dynamic-slice_fusion.10
  475.5 3.4 dynamic-slice_bitcast_fusion
  481.7 7.1 reshape.420
  495.2 6.8 copy.73
  502.0 2.7 constant_dynamic-slice_fusion.1
  504.7 3.0 convolution_convert_fusion.3
  507.7 3.0 convolution_convert_fusion.2
  510.7 3.7 fusion.56
  514.4 9.3 %constant_dynamic-slice_fusion.4 = (bf16[512,1,2176]{2,1,0:T(2,128)(2,1)S(1)}, bf16[512,1,2176]{2,1,0:T(2,128)(2,1)S(1)}) fusion(bf16[512,2,2176]{2,1,0:T(2,128)(2,1)S(1)} %bitcast.241, s32[]{:T(128)S(6)} %select_n.144, s32[]{:T(128)S(6)} %select_n.148), kind=kLoop, calls=%fused_computation.166 | loop fusion | bytes 8912904 | tf_op jit(solution)/shard_map/jit(dynamic_index_in_dim)/dynamic_slice | solution.py:157
  526.0 3.0 convolution_convert_fusion
  529.2 3.0 convolution_convert_fusion.1
  532.3 3.8 fusion.45
  537.6 13.9 %fusion.18 = f32[1,512,1088]{1,2,0:T(8,128)} fusion(f32[512,1088]{0,1:T(8,128)S(1)} %copy-done.6, bf16[512,4352]{1,0:T(8,128)(2,1)} %get-tuple-element.86, bf16[4352,1088]{1,0:T(8,128)(2,1)} %all-gather.15.cloned.1.call-done, f32[1088]{0:T(1024)S(1)} %copy-done.59), kind=kOutput, calls=%fused_computation.35 | convolution fusion | flops 4849729536 | bytes 18387200 | tf_op jit(solution)/shard_map/dot_general | solution.py:18
  565.3 2.9 add_convert_fusion.6
  568.2 4.6 collective-permute-start.10
  574.7 3.0 convert_reduce_fusion.1
  577.6 10.5 %collective-permute-done = bf16[1,512,1088]{1,2,0:T(8,128)(2,1)} collective-permute-done((bf16[1,512,1088]{1,2,0:T(8,128)(2,1)}, bf16[1,512,1088]{1,2,0:T(8,128)(2,1)}, u32[]{:S(2)}, u32[]{:S(2)}) %collective-permute-start) | collective-permute-done | bytes 1114144 | tf_op jit(solution)/shard_map/ppermute | solution.py:279
  590.6 3.4 fusion.41
  593.9 6.7 concatenate.22
  600.6 5.6 copy.66
  606.2 4.2 convolution_convert_fusion.4
  610.5 6.6 fusion.107
  619.5 2.8 reshape.406
  622.3 4.5 add_bitcast_fusion
  626.8 2.6 convolution_convert_fusion.5
  631.0 4.8 add_convert_fusion.1
  635.8 85.4 %all-reduce.14 = f32[32,408]{1,0:T(8,128)S(1)} all-reduce(f32[32,408]{1,0:T(8,128)S(1)} %pad_maximum_fusion.2), channel_id=6, replica_groups=mesh['dp'=16,'seq'=2] {'dp','seq'}, use_global_device_ids=true, to_apply=%region_17.18.clone | all-reduce | flops 13056 | bytes 104448
  722.7 3.0 convert_add_fusion.3
  725.7 3.2 copy.69
  732.4 4.4 fusion.33
  736.7 3.4 collective-permute-done.11
  741.8 4.3 add_convert_fusion.2
  747.8 4.7 add_convert_fusion
  754.6 5.3 convert_add_fusion.1
  760.0 6.1 copy.74
  769.9 21.1 %collective-permute-done.4 = bf16[576,1632]{1,0:T(8,128)(2,1)} collective-permute-done((bf16[576,1632]{1,0:T(8,128)(2,1)}, bf16[576,1632]{1,0:T(8,128)(2,1)}, u32[]{:S(2)}, u32[]{:S(2)}) %collective-permute-start.4) | collective-permute-done | bytes 1880096 | tf_op jit(solution)/shard_map/ppermute | solution.py:143
  791.0 3.8 convert_add_fusion.2
  797.6 46.6 %collective-permute-done.16 = bf16[576,2176]{1,0:T(8,128)(2,1)} collective-permute-done((bf16[576,2176]{1,0:T(8,128)(2,1)}, bf16[576,2176]{1,0:T(8,128)(2,1)}, u32[]{:S(2)}, u32[]{:S(2)}) %collective-permute-start.16) | collective-permute-done | bytes 2506784 | tf_op jit(solution)/shard_map/ppermute | solution.py:143
  851.9 23.8 %collective-permute-done.17 = bf16[4,72,2176]{2,1,0:T(8,128)(2,1)S(1)} collective-permute-done((bf16[4,72,2176]{2,1,0:T(8,128)(2,1)S(1)}, bf16[4,72,2176]{2,1,0:T(8,128)(2,1)S(1)}, u32[]{:S(2)}, u32[]{:S(2)}) %collective-permute-start.17) | collective-permute-done | bytes 1253408 | tf_op jit(solution)/shard_map/ppermute | solution.py:143
  879.9 23.5 %collective-permute-done.18 = bf16[2,72,2176]{2,1,0:T(8,128)(2,1)S(1)} collective-permute-done((bf16[2,72,2176]{2,1,0:T(8,128)(2,1)S(1)}, bf16[2,72,2176]{2,1,0:T(8,128)(2,1)S(1)}, u32[]{:S(2)}, u32[]{:S(2)}) %collective-permute-start.18) | collective-permute-done | bytes 626720 | tf_op jit(solution)/shard_map/ppermute | solution.py:143
  905.4 13.0 %collective-permute-done.19 = bf16[1,72,2176]{2,1,0:T(8,128)(2,1)S(1)} collective-permute-done((bf16[1,72,2176]{2,1,0:T(8,128)(2,1)S(1)}, bf16[1,72,2176]{2,1,0:T(8,128)(2,1)S(1)}, u32[]{:S(2)}, u32[]{:S(2)}) %collective-permute-start.19) | collective-permute-done | bytes 313376 | tf_op jit(solution)/shard_map/ppermute | solution.py:143
  (320 shorter events, 113.6 us)
Async XLA Ops:
  7.2 74.2 %copy-start.2 = (f32[1,512,1088]{1,2,0:T(8,128)S(1)}, f32[1,512,1088]{1,2,0:T(8,128)}, u32[]{:S(2)}) copy-start(f32[1,512,1088]{1,2,0:T(8,128)} %param.8) | copy-start | bytes 6684676
  7.2 133.1 %all-gather.11.cloned.1.call-start = ((), (), s32[]{:S(2)}) async-start(), calls=%async_computation.1 | async-start | bytes 3342336 | tf_op jit(solution)/shard_map/all_gather | solution.py:232
  83.3 9.6 %copy-start.34 = (f32[68,2176]{1,0:T(8,128)S(1)}, f32[68,2176]{1,0:T(8,128)}, u32[]{:S(2)}) copy-start(f32[68,2176]{1,0:T(8,128)} %param.11) | copy-start | bytes 1775620
  83.3 118.2 %all-gather.9.cloned.1.call-start = ((), (), s32[]{:S(2)}) async-start(), calls=%async_computation | async-start | bytes 8146944 | tf_op jit(solution)/shard_map/all_gather | solution.py:212
  83.4 9.5 %copy-start.40 = (f32[68,544]{1,0:T(8,128)S(1)}, f32[68,544]{1,0:T(8,128)}, u32[]{:S(2)}) copy-start(f32[68,544]{1,0:T(8,128)} %param.10) | copy-start | bytes 443908
  92.8 211.3 %all-gather.13.cloned.1.call-start = ((), (), s32[]{:S(2)}) async-start(), calls=%async_computation.2 | async-start | bytes 13473792 | tf_op jit(solution)/shard_map/all_gather | solution.py:212
  101.2 18.6 %copy-start.33 = (f32[272,544]{1,0:T(8,128)S(1)}, f32[272,544]{1,0:T(8,128)}, u32[]{:S(2)}) copy-start(f32[272,544]{1,0:T(8,128)} %param.12) | copy-start | bytes 1775620
  119.7 270.2 %all-gather.15.cloned.1.call-start = ((), (), s32[]{:S(2)}) async-start(), calls=%async_computation.3 | async-start | bytes 10653696 | tf_op jit(solution)/shard_map/all_gather | solution.py:212
  119.8 11.7 %copy-start.43 = (f32[1088]{0:T(1024)S(1)}, f32[1088]{0:T(1024)}, u32[]{:S(2)}) copy-start(f32[1088]{0:T(1024)} %copy-done.42) | copy-start | bytes 13060
  119.8 11.8 %copy-start.48 = (f32[1088]{0:T(1024)S(1)}, f32[1088]{0:T(1024)}, u32[]{:S(2)}) copy-start(f32[1088]{0:T(1024)} %copy-done.47) | copy-start | bytes 13060
  205.3 16.3 %copy-start = (bf16[1,512,1152]{2,1,0:T(8,128)(2,1)}, bf16[1,512,1152]{2,1,0:T(8,128)(2,1)S(1)}, u32[]{:S(2)}) copy-start(bf16[1,512,1152]{2,1,0:T(8,128)(2,1)S(1)} %pad.62.q_ref) | copy-start | bytes 3538948
  207.3 9.4 %copy-start.56 = (f32[1088]{0:T(1024)S(1)}, f32[1088]{0:T(1024)}, u32[]{:S(2)}) copy-start(f32[1088]{0:T(1024)} %get-tuple-element.54) | copy-start | bytes 13060
  404.0 9.7 %copy-start.22 = (bf16[512,4352]{1,0:T(8,128)(2,1)}, bf16[512,4352]{1,0:T(8,128)(2,1)S(1)}, u32[]{:S(2)}) copy-start(bf16[512,4352]{1,0:T(8,128)(2,1)S(1)} %get-tuple-element.89) | copy-start | bytes 13369348
  493.7 74.5 %collective-permute-start.1 = (bf16[1,512,1088]{1,2,0:T(8,128)(2,1)}, bf16[1,512,1088]{1,2,0:T(8,128)(2,1)}, u32[]{:S(2)}, u32[]{:S(2)}) collective-permute-start(bf16[1,512,1088]{1,2,0:T(8,128)(2,1)} %slice.217), channel_id=1, source_target_pairs={{1,0},{3,2},{5,4},{7,6},{9,8},{11,10},{13,12},{15,14},{17,16},{19,... | collective-permute-start | bytes 3342344 | tf_op jit(solution)/shard_map/ppermute | solution.py:279
  504.7 6.0 copy-start.11
  514.4 9.4 %copy-start.16 = (bf16[512,16,72]{0,2,1:T(8,128)(2,1)S(1)}, bf16[512,16,72]{0,2,1:T(8,128)(2,1)}, u32[]{:S(2)}) copy-start(bf16[512,16,72]{0,2,1:T(8,128)(2,1)} %pad.74) | copy-start | bytes 3538948
  514.4 9.4 %copy-start.18 = (bf16[512,16,72]{0,2,1:T(8,128)(2,1)S(1)}, bf16[512,16,72]{0,2,1:T(8,128)(2,1)}, u32[]{:S(2)}) copy-start(bf16[512,16,72]{0,2,1:T(8,128)(2,1)} %copy-done.17) | copy-start | bytes 3538948
  525.0 7.3 copy-start.23
  525.0 11.1 %copy-start.35 = (bf16[512,8,1,72]{0,3,2,1:T(8,128)(2,1)}, bf16[512,8,1,72]{0,3,2,1:T(8,128)(2,1)S(1)}, u32[]{:S(2)}) copy-start(bf16[512,8,1,72]{0,3,2,1:T(8,128)(2,1)S(1)} %get-tuple-element.92) | copy-start | bytes 1769476
  529.0 217.1 %collective-permute-start.15 = (bf16[576,2176]{1,0:T(8,128)(2,1)}, bf16[576,2176]{1,0:T(8,128)(2,1)}, u32[]{:S(2)}, u32[]{:S(2)}) collective-permute-start(bf16[576,2176]{1,0:T(8,128)(2,1)} %convolution_convert_fusion), channel_id=1, source_target_pairs={{0,2},{2,0},{4,6},{6,4},{8,10},{10,8},{12,14},{14,12},{16,18},{18,... | collective-permute-start | bytes 7520264 | tf_op jit(solution)/shard_map/ppermute | solution.py:143
  532.3 5.3 copy-start.6
  532.3 5.3 copy-start.59
  537.6 13.9 %copy-start.36 = (bf16[512,8,1,72]{0,3,2,1:T(8,128)(2,1)S(1)}, bf16[512,8,1,72]{0,3,2,1:T(8,128)(2,1)}, u32[]{:S(2)}) copy-start(bf16[512,8,1,72]{0,3,2,1:T(8,128)(2,1)} %copy-done.35) | copy-start | bytes 1769476
  557.8 30.4 %collective-permute-start = (bf16[1,512,1088]{1,2,0:T(8,128)(2,1)}, bf16[1,512,1088]{1,2,0:T(8,128)(2,1)}, u32[]{:S(2)}, u32[]{:S(2)}) collective-permute-start(bf16[1,512,1088]{1,2,0:T(8,128)(2,1)} %slice.215), channel_id=1, source_target_pairs={{1,0},{3,2},{5,4},{7,6},{9,8},{11,10},{13,12},{15,14},{17,16},{19,... | collective-permute-start | bytes 3342344 | tf_op jit(solution)/shard_map/ppermute | solution.py:279
  559.1 71.6 %collective-permute-start.21 = (bf16[2176,544]{0,1:T(8,128)(2,1)}, bf16[2176,544]{0,1:T(8,128)(2,1)}, u32[]{:S(2)}, u32[]{:S(2)}) collective-permute-start(bf16[2176,544]{0,1:T(8,128)(2,1)} %convolution_convert_fusion.2), channel_id=1, source_target_pairs={{0,2},{2,0},{4,6},{6,4},{8,10},{10,8},{12,14},{14,12},{16,18},{18,... | collective-permute-start | bytes 7102472 | tf_op jit(solution)/shard_map/ppermute | solution.py:143
  559.4 5.7 collective-permute-start.9
  565.1 70.8 %collective-permute-start.8 = (bf16[576,544]{0,1:T(8,128)(2,1)}, bf16[576,544]{0,1:T(8,128)(2,1)}, u32[]{:S(2)}, u32[]{:S(2)}) collective-permute-start(bf16[576,544]{0,1:T(8,128)(2,1)} %convolution_convert_fusion.8), channel_id=1, source_target_pairs={{0,2},{2,0},{4,6},{6,4},{8,10},{10,8},{12,14},{14,12},{16,18},{18,... | collective-permute-start | bytes 1880072 | tf_op jit(solution)/shard_map/ppermute | solution.py:143
  568.2 154.4 %collective-permute-start.10 = (bf16[576,544]{0,1:T(8,128)(2,1)}, bf16[576,544]{0,1:T(8,128)(2,1)}, u32[]{:S(2)}, u32[]{:S(2)}) collective-permute-start(bf16[576,544]{0,1:T(8,128)(2,1)} %add_convert_fusion.6), channel_id=1, source_target_pairs={{0,1},{1,0},{2,3},{3,2},{4,5},{5,4},{6,7},{7,6},{8,9},{9,8},{10,11... | collective-permute-start | bytes 1880072 | tf_op jit(solution)/shard_map/ppermute | solution.py:143
  600.6 5.6 copy-start.37
  610.4 6.7 copy-start.7
  610.4 6.7 copy-start.46
  610.4 6.7 copy-start.51
  610.4 6.7 copy-start.54
  610.4 129.9 %collective-permute-start.3 = (bf16[576,1632]{1,0:T(8,128)(2,1)}, bf16[576,1632]{1,0:T(8,128)(2,1)}, u32[]{:S(2)}, u32[]{:S(2)}) collective-permute-start(bf16[576,1632]{1,0:T(8,128)(2,1)} %convolution_convert_fusion.4), channel_id=1, source_target_pairs={{0,2},{2,0},{4,6},{6,4},{8,10},{10,8},{12,14},{14,12},{16,18},{18,... | collective-permute-start | bytes 5640200 | tf_op jit(solution)/shard_map/ppermute | solution.py:143
  630.7 121.9 %collective-permute-start.20 = (bf16[2176,544]{0,1:T(8,128)(2,1)}, bf16[2176,544]{0,1:T(8,128)(2,1)}, u32[]{:S(2)}, u32[]{:S(2)}) collective-permute-start(bf16[2176,544]{0,1:T(8,128)(2,1)} %convolution_convert_fusion.3), channel_id=1, source_target_pairs={{0,2},{2,0},{4,6},{6,4},{8,10},{10,8},{12,14},{14,12},{16,18},{18,... | collective-permute-start | bytes 7102472 | tf_op jit(solution)/shard_map/ppermute | solution.py:143
  635.8 117.2 %collective-permute-start.22 = (bf16[2176,544]{0,1:T(8,128)(2,1)}, bf16[2176,544]{0,1:T(8,128)(2,1)}, u32[]{:S(2)}, u32[]{:S(2)}) collective-permute-start(bf16[2176,544]{0,1:T(8,128)(2,1)} %add_convert_fusion.1), channel_id=1, source_target_pairs={{0,1},{1,0},{2,3},{3,2},{4,5},{5,4},{6,7},{7,6},{8,9},{9,8},{10,11... | collective-permute-start | bytes 7102472 | tf_op jit(solution)/shard_map/ppermute | solution.py:143
  725.7 6.7 copy-start.15
  730.0 10.1 %collective-permute-start.11 = (bf16[4,72,544]{2,1,0:T(8,128)(2,1)S(1)}, bf16[4,72,544]{2,1,0:T(8,128)(2,1)S(1)}, u32[]{:S(2)}, u32[]{:S(2)}) collective-permute-start(bf16[4,72,544]{2,1,0:T(8,128)(2,1)S(1)} %fusion.76), channel_id=1, source_target_pairs={{0,4},{2,6},{4,0},{6,2},{8,12},{10,14},{12,8},{14,10},{16,20},{18,... | collective-permute-start | bytes 940040 | tf_op jit(solution)/shard_map/ppermute | solution.py:143
  732.4 7.8 copy-start.20
  732.4 9.4 %copy-start.25 = (bf16[512,8,1,72]{0,3,2,1:T(8,128)(2,1)S(1)}, bf16[512,8,1,72]{0,3,2,1:T(8,128)(2,1)}, u32[]{:S(2)}) copy-start(bf16[512,8,1,72]{0,3,2,1:T(8,128)(2,1)} %get-tuple-element.74) | copy-start | bytes 1769476
  740.2 28.0 %collective-permute-start.2 = (bf16[576,1632]{1,0:T(8,128)(2,1)}, bf16[576,1632]{1,0:T(8,128)(2,1)}, u32[]{:S(2)}, u32[]{:S(2)}) collective-permute-start(bf16[576,1632]{1,0:T(8,128)(2,1)} %convolution_convert_fusion.5), channel_id=1, source_target_pairs={{0,2},{2,0},{4,6},{6,4},{8,10},{10,8},{12,14},{14,12},{16,18},{18,... | collective-permute-start | bytes 5640200 | tf_op jit(solution)/shard_map/ppermute | solution.py:143
  740.2 7.6 slice-start.8
  740.3 7.5 slice-start.9
  740.3 7.5 copy-start.24
  740.3 12.2 %collective-permute-start.12 = (bf16[2,72,544]{2,1,0:T(8,128)(2,1)S(1)}, bf16[2,72,544]{2,1,0:T(8,128)(2,1)S(1)}, u32[]{:S(2)}, u32[]{:S(2)}) collective-permute-start(bf16[2,72,544]{2,1,0:T(8,128)(2,1)S(1)} %fusion.77), channel_id=1, source_target_pairs={{0,8},{2,10},{4,12},{6,14},{8,0},{10,2},{12,4},{14,6},{16,24},{18,... | collective-permute-start | bytes 470024 | tf_op jit(solution)/shard_map/ppermute | solution.py:143
  741.8 12.8 %slice-start.4 = ((s8[4734976]{0:T(1024)(128)(4,1)}), s8[4194304]{0:T(1024)(128)(4,1)S(1)}, s32[]{:S(2)}) async-start(s8[4734976]{0:T(1024)(128)(4,1)} %bitcast.246), calls=%async_computation.8 | async-start | bytes 8388608
  746.1 8.6 slice-start.5
  746.1 44.9 %collective-permute-start.4 = (bf16[576,1632]{1,0:T(8,128)(2,1)}, bf16[576,1632]{1,0:T(8,128)(2,1)}, u32[]{:S(2)}, u32[]{:S(2)}) collective-permute-start(bf16[576,1632]{1,0:T(8,128)(2,1)} %add_convert_fusion.2), channel_id=1, source_target_pairs={{0,1},{1,0},{2,3},{3,2},{4,5},{5,4},{6,7},{7,6},{8,9},{9,8},{10,11... | collective-permute-start | bytes 5640200 | tf_op jit(solution)/shard_map/ppermute | solution.py:143
  752.6 45.0 %collective-permute-start.14 = (bf16[576,2176]{1,0:T(8,128)(2,1)}, bf16[576,2176]{1,0:T(8,128)(2,1)S(1)}, u32[]{:S(2)}, u32[]{:S(2)}) collective-permute-start(bf16[576,2176]{1,0:T(8,128)(2,1)} %convolution_convert_fusion.1), channel_id=1, source_target_pairs={{0,2},{2,0},{4,6},{6,4},{8,10},{10,8},{12,14},{14,12},{16,18},{18,... | collective-permute-start | bytes 7520264 | tf_op jit(solution)/shard_map/ppermute | solution.py:143
  752.6 91.5 %collective-permute-start.16 = (bf16[576,2176]{1,0:T(8,128)(2,1)}, bf16[576,2176]{1,0:T(8,128)(2,1)}, u32[]{:S(2)}, u32[]{:S(2)}) collective-permute-start(bf16[576,2176]{1,0:T(8,128)(2,1)} %add_convert_fusion), channel_id=1, source_target_pairs={{0,1},{1,0},{2,3},{3,2},{4,5},{5,4},{6,7},{7,6},{8,9},{9,8},{10,11... | collective-permute-start | bytes 7520264 | tf_op jit(solution)/shard_map/ppermute | solution.py:143
  753.1 95.4 %collective-permute-start.13 = (bf16[1,72,544]{2,1,0:T(8,128)(2,1)S(1)}, bf16[1,72,544]{2,1,0:T(8,128)(2,1)S(1)}, u32[]{:S(2)}, u32[]{:S(2)}) collective-permute-start(bf16[1,72,544]{2,1,0:T(8,128)(2,1)S(1)} %dynamic-slice_convert_fusion.9), channel_id=1, source_target_pairs={{0,16},{2,18},{4,20},{6,22},{8,24},{10,26},{12,28},{14,30},{16,0},... | collective-permute-start | bytes 235016 | tf_op jit(solution)/shard_map/ppermute | solution.py:143
  766.1 78.1 %slice-start.2 = ((s8[5013504]{0:T(1024)(128)(4,1)}), s8[4194304]{0:T(1024)(128)(4,1)S(1)}, s32[]{:S(2)}) async-start(s8[5013504]{0:T(1024)(128)(4,1)} %bitcast.242), calls=%async_computation.6 | async-start | bytes 8388608
  768.2 76.0 %slice-start.3 = ((s8[5013504]{0:T(1024)(128)(4,1)}), s8[819200]{0:T(1024)(128)(4,1)S(1)}, s32[]{:S(2)}) async-start(s8[5013504]{0:T(1024)(128)(4,1)} %bitcast.242), calls=%async_computation.7 | async-start | bytes 1638400
  768.2 81.9 %collective-permute-start.23 = (bf16[4,272,544]{2,1,0:T(8,128)(2,1)S(1)}, bf16[4,272,544]{2,1,0:T(8,128)(2,1)S(1)}, u32[]{:S(2)}, u32[]{:S(2)}) collective-permute-start(bf16[4,272,544]{2,1,0:T(8,128)(2,1)S(1)} %fusion.39), channel_id=1, source_target_pairs={{0,4},{2,6},{4,0},{6,2},{8,12},{10,14},{12,8},{14,10},{16,20},{18,... | collective-permute-start | bytes 3551240 | tf_op jit(solution)/shard_map/ppermute | solution.py:143
  794.7 55.3 %slice-start.6 = ((s8[5570560]{0:T(1024)(128)(4,1)}), s8[4194304]{0:T(1024)(128)(4,1)S(1)}, s32[]{:S(2)}) async-start(s8[5570560]{0:T(1024)(128)(4,1)} %bitcast.250), calls=%async_computation.10 | async-start | bytes 8388608
  795.8 54.3 %slice-start.7 = ((s8[5570560]{0:T(1024)(128)(4,1)}), s8[1376256]{0:T(1024)(128)(4,1)S(1)}, s32[]{:S(2)}) async-start(s8[5570560]{0:T(1024)(128)(4,1)} %bitcast.250), calls=%async_computation.11 | async-start | bytes 2752512
  795.8 53.3 %collective-permute-start.5 = (bf16[4,72,1632]{2,1,0:T(8,128)(2,1)}, bf16[4,72,1632]{2,1,0:T(8,128)(2,1)S(1)}, u32[]{:S(2)}, u32[]{:S(2)}) collective-permute-start(bf16[4,72,1632]{2,1,0:T(8,128)(2,1)} %fusion.44), channel_id=1, source_target_pairs={{0,4},{2,6},{4,0},{6,2},{8,12},{10,14},{12,8},{14,10},{16,20},{18,... | collective-permute-start | bytes 2820104 | tf_op jit(solution)/shard_map/ppermute | solution.py:143
  846.6 29.1 %collective-permute-start.17 = (bf16[4,72,2176]{2,1,0:T(8,128)(2,1)S(1)}, bf16[4,72,2176]{2,1,0:T(8,128)(2,1)S(1)}, u32[]{:S(2)}, u32[]{:S(2)}) collective-permute-start(bf16[4,72,2176]{2,1,0:T(8,128)(2,1)S(1)} %fusion.40), channel_id=1, source_target_pairs={{0,4},{2,6},{4,0},{6,2},{8,12},{10,14},{12,8},{14,10},{16,20},{18,... | collective-permute-start | bytes 3760136 | tf_op jit(solution)/shard_map/ppermute | solution.py:143
  849.4 27.1 %collective-permute-start.6 = (bf16[2,72,1632]{2,1,0:T(8,128)(2,1)S(1)}, bf16[2,72,1632]{2,1,0:T(8,128)(2,1)S(1)}, u32[]{:S(2)}, u32[]{:S(2)}) collective-permute-start(bf16[2,72,1632]{2,1,0:T(8,128)(2,1)S(1)} %fusion.74), channel_id=1, source_target_pairs={{0,8},{2,10},{4,12},{6,14},{8,0},{10,2},{12,4},{14,6},{16,24},{18,... | collective-permute-start | bytes 1410056 | tf_op jit(solution)/shard_map/ppermute | solution.py:143
  850.4 27.7 %collective-permute-start.24 = (bf16[2,272,544]{2,1,0:T(8,128)(2,1)S(1)}, bf16[2,272,544]{2,1,0:T(8,128)(2,1)S(1)}, u32[]{:S(2)}, u32[]{:S(2)}) collective-permute-start(bf16[2,272,544]{2,1,0:T(8,128)(2,1)S(1)} %fusion.47), channel_id=1, source_target_pairs={{0,8},{2,10},{4,12},{6,14},{8,0},{10,2},{12,4},{14,6},{16,24},{18,... | collective-permute-start | bytes 1775624 | tf_op jit(solution)/shard_map/ppermute | solution.py:143
  876.0 27.3 %collective-permute-start.18 = (bf16[2,72,2176]{2,1,0:T(8,128)(2,1)S(1)}, bf16[2,72,2176]{2,1,0:T(8,128)(2,1)S(1)}, u32[]{:S(2)}, u32[]{:S(2)}) collective-permute-start(bf16[2,72,2176]{2,1,0:T(8,128)(2,1)S(1)} %fusion.48), channel_id=1, source_target_pairs={{0,8},{2,10},{4,12},{6,14},{8,0},{10,2},{12,4},{14,6},{16,24},{18,... | collective-permute-start | bytes 1880072 | tf_op jit(solution)/shard_map/ppermute | solution.py:143
  876.6 27.0 %collective-permute-start.7 = (bf16[1,72,1632]{2,1,0:T(8,128)(2,1)S(1)}, bf16[1,72,1632]{2,1,0:T(8,128)(2,1)S(1)}, u32[]{:S(2)}, u32[]{:S(2)}) collective-permute-start(bf16[1,72,1632]{2,1,0:T(8,128)(2,1)S(1)} %dynamic-slice_convert_fusion.7), channel_id=1, source_target_pairs={{0,16},{2,18},{4,20},{6,22},{8,24},{10,26},{12,28},{14,30},{16,0},... | collective-permute-start | bytes 705032 | tf_op jit(solution)/shard_map/ppermute | solution.py:143
  878.3 26.1 %collective-permute-start.25 = (bf16[1,272,544]{2,1,0:T(8,128)(2,1)S(1)}, bf16[1,272,544]{2,1,0:T(8,128)(2,1)S(1)}, u32[]{:S(2)}, u32[]{:S(2)}) collective-permute-start(bf16[1,272,544]{2,1,0:T(8,128)(2,1)S(1)} %dynamic-slice_convert_fusion.5), channel_id=1, source_target_pairs={{0,16},{2,18},{4,20},{6,22},{8,24},{10,26},{12,28},{14,30},{16,0},... | collective-permute-start | bytes 887816 | tf_op jit(solution)/shard_map/ppermute | solution.py:143
  903.5 14.8 %collective-permute-start.19 = (bf16[1,72,2176]{2,1,0:T(8,128)(2,1)S(1)}, bf16[1,72,2176]{2,1,0:T(8,128)(2,1)S(1)}, u32[]{:S(2)}, u32[]{:S(2)}) collective-permute-start(bf16[1,72,2176]{2,1,0:T(8,128)(2,1)S(1)} %dynamic-slice_convert_fusion.6), channel_id=1, source_target_pairs={{0,16},{2,18},{4,20},{6,22},{8,24},{10,26},{12,28},{14,30},{16,0},... | collective-permute-start | bytes 940040 | tf_op jit(solution)/shard_map/ppermute | solution.py:143
  (37 other events, 105.1 us)
Sparse Core Ops, SparseCore 0:
  83.4 44.0 all-gather.10
  130.2 71.2 all-gather.8
  204.3 99.7 all-gather.12
  306.7 83.2 all-gather.14

commit v2 on v1

--- a/solution.py
+++ b/solution.py
@@ -197,6 +197,13 @@
     x = inputs.reshape(tokens, width)
     cot = cotangent.reshape(tokens, width)
 
+    def columns(weight):
+        pieces = lax.all_gather(pad_rows(weight.astype(BF)), "seq", axis=0)
+        return jnp.concatenate([pieces[i] for i in range(seq)], -1)
+
+    attend_cols, vectors, up_bias = lax.optimization_barrier(
+        (columns(attend_weight), vectors, up_bias)
+    )
     few = jnp.concatenate([vectors.astype(BF).reshape(-1), up_bias.astype(BF)])
     filled = jnp.pad(few, (0, -few.size % 1024)).reshape(-1, 128)
     few = lax.all_gather(filled, ("dp", "seq"), axis=0, tiled=True).reshape(dp * seq, -1)
@@ -204,14 +211,10 @@
     vec = vec.transpose(1, 3, 0, 2).reshape(8, width).astype(F32)
     bias = few[:, vectors.size : vectors.size + up_bias.size].reshape(-1).astype(F32)
 
-    def columns(weight):
-        pieces = lax.all_gather(pad_rows(weight.astype(BF)), "seq", axis=0)
-        return jnp.concatenate([pieces[i] for i in range(seq)], -1)
-
     def whole(part):
         return lax.all_gather(part, "dp", axis=0, tiled=True)
 
-    attend_full = whole(columns(attend_weight))
+    attend_full = whole(attend_cols)
     out_cols, up_cols = columns(out_weight), columns(up_weight)
     joint = whole(jnp.concatenate([out_cols, up_cols], -1))
     out_full, up_full = joint[:, :width], joint[:, width:]

time: 932 us -> 937 us (level)
  no operation moved by 1% of the time
where the time goes in v2:
time: 937 us; the launch traced here: 930 us
  waiting for transfers between devices  308 us (33%)
  blocking collectives  201 us (21%)
  local copies, waits for them, and re-layouts  133 us (14%)
  matrix products  130 us (14%)
  Pallas kernels  63.4 us (7%)
  other arithmetic  52.4 us (6%)
  starting transfers between devices  27.4 us (3%)
  between operations  15 us (2%)
    all_gather x3, waiting for transfers between devices, whole(): return lax.all_gather(part, 'dp', axis=0, tiled=True)  163 us
    ppermute x24, waiting for transfers between devices, exchange(): return lax.ppermute(value, axis, [(i, i ^ stride) for i in range(size)])  134 us
    dot_general x25, matrix products, dot(): lax.dot_general(left, right, (dims, ((), ())), preferred_element_type=F32)  130 us
    unnamed x1, blocking collectives  85.4 us
    all_gather x1, blocking collectives, body(): lax.all_gather(filled, ('dp', 'seq'), axis=0, tiled=True)  67.9 us
    all_gather x4, blocking collectives, columns(): pieces = lax.all_gather(pad_rows(weight.astype(BF)), 'seq', axis=0)  48.1 us
    pallas_call x1, Pallas kernels, attend_back(): pl.pallas_call(attend_back_kernel, grid=(seqs, pairs), in_specs=[small, l...  37.1 us
    pallas_call x1, Pallas kernels, attend(): pl.pallas_call(attend_kernel, grid=(seqs, pairs), in_specs=[small, large,...  26.3 us
  transfers between devices with their start and end apart: 30, of which 11 were waited for; matrix products, arithmetic and copies ran while one was open for 25% of the time, Pallas kernels for 3%

profile of v2, /device:TPU:0, one launch (start us, length us, event | category | flops | bytes accessed | tf_op | source)
XLA Modules:
  0.0 930.2 jit_solution(4894691212932451980)
XLA Ops:
  8.3 9.5 %all-gather = bf16[144,1632]{1,0:T(8,128)(2,1)S(1)} all-gather(bf16[72,1632]{1,0:T(8,128)(2,1)S(1)} %pad.59), channel_id=2, replica_groups=mesh['dp'=16,'seq'=2] {'seq'}, dimensions={0}, use_global_device_ids=true | all-gather | bytes 705024 | tf_op jit(solution)/shard_map/all_gather | solution.py:201
  19.1 67.9 %all_gather.41 = bf16[256,128]{1,0:T(8,128)(2,1)S(1)} all-gather(bf16[8,128]{1,0:T(8,128)(2,1)S(1)} %fusion.94), channel_id=1, replica_groups=mesh['dp'=16,'seq'=2] {'dp','seq'}, dimensions={0}, use_global_device_ids=true | all-gather | bytes 67584 | tf_op jit(solution)/shard_map/all_gather | solution.py:209
  92.7 6.2 all-gather.1
  98.9 15.6 %all-gather.2 = bf16[144,2176]{1,0:T(8,128)(2,1)S(1)} all-gather(bf16[72,2176]{1,0:T(8,128)(2,1)S(1)} %pad.67), channel_id=4, replica_groups=mesh['dp'=16,'seq'=2] {'seq'}, dimensions={0}, use_global_device_ids=true | all-gather | bytes 940032 | tf_op jit(solution)/shard_map/all_gather | solution.py:201
  117.7 16.8 %all-gather.3 = bf16[544,544]{1,0:T(8,128)(2,1)S(1)} all-gather(bf16[272,544]{1,0:T(8,128)(2,1)S(1)} %convert_element_type.311), channel_id=5, replica_groups=mesh['dp'=16,'seq'=2] {'seq'}, dimensions={0}, use_global_device_ids=true | all-gather | bytes 887808 | tf_op jit(solution)/shard_map/all_gather | solution.py:201
  144.4 2.7 reshape_reshape.21
  149.0 56.7 %all-gather.9.cloned.1.call-done = bf16[1152,3264]{1,0:T(8,128)(2,1)} async-done(((bf16[72,3264]{1,0:T(8,128)(2,1)}), bf16[1152,3264]{1,0:T(8,128)(2,1)}) %all-gather.9.cloned.1.call-update) | async-done | bytes 7520272 | tf_op jit(solution)/shard_map/all_gather | solution.py:215
  205.7 3.6 fusion.21
  211.4 9.4 %fusion.13 = f32[1024,2176]{1,0:T(8,128)S(1)} fusion(bf16[1024,1152]{0,1:T(8,128)(2,1)S(1)} %bitcast.300, bf16[1152,3264]{1,0:T(8,128)(2,1)} %all-gather.9.cloned.1.call-done), kind=kOutput, calls=%fused_computation.15 | convolution fusion | flops 5133828096 | bytes 16285696 | tf_op jit(solution)/shard_map/dot_general | solution.py:18
  225.7 26.3 %shard_map.143 = (bf16[1,512,1152]{2,1,0:T(8,128)(2,1)S(1)}, f32[1,512,1152]{2,1,0:T(8,128)S(1)}) custom-call(bf16[1,512,1152]{2,1,0:T(8,128)(2,1)S(1)} %pad.62.q_ref, bf16[1,1024,1152]{2,1,0:T(8,128)(2,1)} %pad.64.k_ref, bf16[1,1024,1152]{2,1,0:T(8,128)(2,1)} %pad.65.v_ref), custom_call_target="tpu_custom_call" | custom-call | flops 9663676416 | bytes 9437184 | tf_op jit(solution)/shard_map/pallas_call | solution.py:102
  257.2 51.0 %all-gather.13.cloned.1.call-done = bf16[1152,5440]{1,0:T(8,128)(2,1)} async-done(((bf16[72,5440]{1,0:T(8,128)(2,1)}), bf16[1152,5440]{1,0:T(8,128)(2,1)}) %all-gather.13.cloned.1.call-update) | async-done | bytes 12533776 | tf_op jit(solution)/shard_map/all_gather | solution.py:215
  308.2 3.5 slice.203
  311.7 4.6 reshape.390
  316.3 3.6 fusion.104
  325.1 13.5 %multiply_convert_fusion = (bf16[512,4352]{1,0:T(8,128)(2,1)}, f32[512,4352]{1,0:T(8,128)}) fusion(f32[4352]{0:T(1024)S(1)} %copy-done.56, bf16[512,1152]{0,1:T(8,128)(2,1)S(1)} %bitcast.270, bf16[1152,5440]{1,0:T(8,128)(2,1)} %all-gather.13.cloned.1.call-done), kind=kOutput, calls=%fused_computation.8 | convolution fusion | flops 5147197440 | bytes 24593408 | tf_op jit(solution)/shard_map/dot_general | solution.py:18
  338.6 55.5 %all-gather.15.cloned.1.call-done = bf16[4352,1088]{1,0:T(8,128)(2,1)} async-done(((bf16[272,1088]{1,0:T(8,128)(2,1)}), bf16[4352,1088]{1,0:T(8,128)(2,1)}) %all-gather.15.cloned.1.call-update) | async-done | bytes 9469968 | tf_op jit(solution)/shard_map/all_gather | solution.py:215
  394.1 14.1 %convert_reduce_fusion = (f32[4352]{0:T(1024)S(1)}, bf16[512,4352]{1,0:T(8,128)(2,1)S(1)}) fusion(bf16[4352,1088]{1,0:T(8,128)(2,1)} %all-gather.15.cloned.1.call-done, f32[512,4352]{1,0:T(8,128)} %get-tuple-element.93, f32[1,512,1088]{1,2,0:T(8,128)} %param.15), kind=kOutput, calls=%fused_computation.7 | convolution fusion | flops 4875350016 | bytes 25084928 | tf_op jit(solution)/shard_map/dot_general | solution.py:18
  408.2 9.7 %fusion.6 = f32[512,1152]{0,1:T(8,128)S(1)} fusion(bf16[512,4352]{1,0:T(8,128)(2,1)S(1)} %get-tuple-element.95, bf16[1152,5440]{1,0:T(8,128)(2,1)} %all-gather.13.cloned.1.call-done), kind=kOutput, calls=%fused_computation.10 | convolution fusion | flops 5133828096 | bytes 16842752 | tf_op jit(solution)/shard_map/dot_general | solution.py:18
  419.6 2.7 reshape.396
  422.3 3.2 multiply_reduce_fusion.3
  430.1 5.0 reshape.398
  435.1 3.6 fusion.20
  439.8 37.1 %shard_map.144 = (bf16[1,512,1152]{2,1,0:T(8,128)(2,1)S(1)}, f32[1,1024,1152]{2,1,0:T(8,128)}, f32[1,1024,1152]{2,1,0:T(8,128)}) custom-call(bf16[1,512,1152]{2,1,0:T(8,128)(2,1)} %copy-done, bf16[1,1024,1152]{2,1,0:T(8,128)(2,1)} %pad.64.k_ref, bf16[1,1024,1152]{2,1,0:T(8,128)(2,1)} %pad.65.v_ref, bf16[1,512,1152]{2,1,0:T(8,128)(2,1)} %pad.69.g_ref, ...), custom_call_target="tpu_custom_call" | custom-call | flops 24159191040 | bytes 20054016 | tf_op jit(solution)/shard_map/pallas_call | solution.py:125
  476.9 2.8 constant_dynamic-slice_fusion.10
  479.7 3.4 dynamic-slice_bitcast_fusion
  485.9 7.1 reshape.420
  499.4 6.8 copy.73
  506.1 2.7 constant_dynamic-slice_fusion.1
  508.9 3.0 convolution_convert_fusion.3
  511.9 3.0 convolution_convert_fusion.2
  514.9 3.7 fusion.56
  518.6 9.3 %constant_dynamic-slice_fusion.4 = (bf16[512,1,2176]{2,1,0:T(2,128)(2,1)S(1)}, bf16[512,1,2176]{2,1,0:T(2,128)(2,1)S(1)}) fusion(bf16[512,2,2176]{2,1,0:T(2,128)(2,1)S(1)} %bitcast.241, s32[]{:T(128)S(6)} %select_n.144, s32[]{:T(128)S(6)} %select_n.148), kind=kLoop, calls=%fused_computation.166 | loop fusion | bytes 8912904 | tf_op jit(solution)/shard_map/jit(dynamic_index_in_dim)/dynamic_slice | solution.py:157
  530.2 3.0 convolution_convert_fusion
  533.4 3.0 convolution_convert_fusion.1
  536.5 3.8 fusion.45
  541.8 13.9 %fusion.18 = f32[1,512,1088]{1,2,0:T(8,128)} fusion(f32[512,1088]{0,1:T(8,128)S(1)} %copy-done.6, bf16[512,4352]{1,0:T(8,128)(2,1)} %get-tuple-element.92, bf16[4352,1088]{1,0:T(8,128)(2,1)} %all-gather.15.cloned.1.call-done, f32[1088]{0:T(1024)S(1)} %copy-done.58), kind=kOutput, calls=%fused_computation.35 | convolution fusion | flops 4849729536 | bytes 18387200 | tf_op jit(solution)/shard_map/dot_general | solution.py:18
  569.5 2.9 add_convert_fusion.6
  572.4 4.6 collective-permute-start.10
  578.9 3.0 convert_reduce_fusion.1
  581.9 10.5 %collective-permute-done = bf16[1,512,1088]{1,2,0:T(8,128)(2,1)} collective-permute-done((bf16[1,512,1088]{1,2,0:T(8,128)(2,1)}, bf16[1,512,1088]{1,2,0:T(8,128)(2,1)}, u32[]{:S(2)}, u32[]{:S(2)}) %collective-permute-start) | collective-permute-done | bytes 1114144 | tf_op jit(solution)/shard_map/ppermute | solution.py:282
  594.8 3.4 fusion.41
  598.1 6.7 concatenate.22
  604.8 5.6 copy.66
  610.4 4.2 convolution_convert_fusion.4
  614.7 6.6 fusion.107
  623.8 2.8 reshape.406
  626.5 4.5 add_bitcast_fusion
  631.0 2.6 convolution_convert_fusion.5
  635.3 4.8 add_convert_fusion.1
  640.1 85.4 %all-reduce.14 = f32[32,408]{1,0:T(8,128)S(1)} all-reduce(f32[32,408]{1,0:T(8,128)S(1)} %pad_maximum_fusion.2), channel_id=6, replica_groups=mesh['dp'=16,'seq'=2] {'dp','seq'}, use_global_device_ids=true, to_apply=%region_17.18.clone | all-reduce | flops 13056 | bytes 104448
  726.9 3.0 convert_add_fusion.3
  730.0 3.2 copy.69
  736.6 4.3 fusion.33
  741.0 3.4 collective-permute-done.11
  746.1 4.3 add_convert_fusion.2
  752.1 4.7 add_convert_fusion
  758.9 5.3 convert_add_fusion.1
  764.3 6.1 copy.74
  774.2 21.1 %collective-permute-done.4 = bf16[576,1632]{1,0:T(8,128)(2,1)} collective-permute-done((bf16[576,1632]{1,0:T(8,128)(2,1)}, bf16[576,1632]{1,0:T(8,128)(2,1)}, u32[]{:S(2)}, u32[]{:S(2)}) %collective-permute-start.4) | collective-permute-done | bytes 1880096 | tf_op jit(solution)/shard_map/ppermute | solution.py:143
  795.3 3.8 convert_add_fusion.2
  801.9 46.5 %collective-permute-done.16 = bf16[576,2176]{1,0:T(8,128)(2,1)} collective-permute-done((bf16[576,2176]{1,0:T(8,128)(2,1)}, bf16[576,2176]{1,0:T(8,128)(2,1)}, u32[]{:S(2)}, u32[]{:S(2)}) %collective-permute-start.16) | collective-permute-done | bytes 2506784 | tf_op jit(solution)/shard_map/ppermute | solution.py:143
  856.2 23.8 %collective-permute-done.17 = bf16[4,72,2176]{2,1,0:T(8,128)(2,1)S(1)} collective-permute-done((bf16[4,72,2176]{2,1,0:T(8,128)(2,1)S(1)}, bf16[4,72,2176]{2,1,0:T(8,128)(2,1)S(1)}, u32[]{:S(2)}, u32[]{:S(2)}) %collective-permute-start.17) | collective-permute-done | bytes 1253408 | tf_op jit(solution)/shard_map/ppermute | solution.py:143
  884.1 23.5 %collective-permute-done.18 = bf16[2,72,2176]{2,1,0:T(8,128)(2,1)S(1)} collective-permute-done((bf16[2,72,2176]{2,1,0:T(8,128)(2,1)S(1)}, bf16[2,72,2176]{2,1,0:T(8,128)(2,1)S(1)}, u32[]{:S(2)}, u32[]{:S(2)}) %collective-permute-start.18) | collective-permute-done | bytes 626720 | tf_op jit(solution)/shard_map/ppermute | solution.py:143
  909.6 13.0 %collective-permute-done.19 = bf16[1,72,2176]{2,1,0:T(8,128)(2,1)S(1)} collective-permute-done((bf16[1,72,2176]{2,1,0:T(8,128)(2,1)S(1)}, bf16[1,72,2176]{2,1,0:T(8,128)(2,1)S(1)}, u32[]{:S(2)}, u32[]{:S(2)}) %collective-permute-start.19) | collective-permute-done | bytes 313376 | tf_op jit(solution)/shard_map/ppermute | solution.py:143
  (322 shorter events, 114.3 us)
Async XLA Ops:
  7.2 11.6 %copy-start.60 = (f32[68,4]{0,1:T(4,128)S(1)}, f32[68,4]{0,1:T(4,128)}, u32[]{:S(2)}) copy-start(f32[68,4]{0,1:T(4,128)} %param.13) | copy-start | bytes 3268
  7.2 11.8 %copy-start.61 = (f32[136]{0:T(256)S(1)}, f32[136]{0:T(256)}, u32[]{:S(2)}) copy-start(f32[136]{0:T(256)} %param.14) | copy-start | bytes 1636
  7.2 137.2 %all-gather.11.cloned.1.call-start = ((), (), s32[]{:S(2)}) async-start(), calls=%async_computation.1 | async-start | bytes 3342336 | tf_op jit(solution)/shard_map/all_gather | solution.py:235
  17.8 71.5 %copy-start.2 = (f32[1,512,1088]{1,2,0:T(8,128)S(1)}, f32[1,512,1088]{1,2,0:T(8,128)}, u32[]{:S(2)}) copy-start(f32[1,512,1088]{1,2,0:T(8,128)} %param.8) | copy-start | bytes 6684676
  91.8 113.9 %all-gather.9.cloned.1.call-start = ((), (), s32[]{:S(2)}) async-start(), calls=%async_computation | async-start | bytes 8146944 | tf_op jit(solution)/shard_map/all_gather | solution.py:215
  92.5 215.7 %all-gather.13.cloned.1.call-start = ((), (), s32[]{:S(2)}) async-start(), calls=%async_computation.2 | async-start | bytes 13473792 | tf_op jit(solution)/shard_map/all_gather | solution.py:215
  98.9 18.7 %copy-start.33 = (f32[272,544]{1,0:T(8,128)S(1)}, f32[272,544]{1,0:T(8,128)}, u32[]{:S(2)}) copy-start(f32[272,544]{1,0:T(8,128)} %param.12) | copy-start | bytes 1775620
  117.6 276.5 %all-gather.15.cloned.1.call-start = ((), (), s32[]{:S(2)}) async-start(), calls=%async_computation.3 | async-start | bytes 10653696 | tf_op jit(solution)/shard_map/all_gather | solution.py:215
  117.7 17.9 %copy-start.42 = (f32[1088]{0:T(1024)S(1)}, f32[1088]{0:T(1024)}, u32[]{:S(2)}) copy-start(f32[1088]{0:T(1024)} %copy-done.41) | copy-start | bytes 13060
  117.7 18.0 %copy-start.47 = (f32[1088]{0:T(1024)S(1)}, f32[1088]{0:T(1024)}, u32[]{:S(2)}) copy-start(f32[1088]{0:T(1024)} %copy-done.46) | copy-start | bytes 13060
  209.4 16.3 %copy-start = (bf16[1,512,1152]{2,1,0:T(8,128)(2,1)}, bf16[1,512,1152]{2,1,0:T(8,128)(2,1)S(1)}, u32[]{:S(2)}) copy-start(bf16[1,512,1152]{2,1,0:T(8,128)(2,1)S(1)} %pad.62.q_ref) | copy-start | bytes 3538948
  211.4 9.4 %copy-start.55 = (f32[1088]{0:T(1024)S(1)}, f32[1088]{0:T(1024)}, u32[]{:S(2)}) copy-start(f32[1088]{0:T(1024)} %get-tuple-element.60) | copy-start | bytes 13060
  408.2 9.7 %copy-start.22 = (bf16[512,4352]{1,0:T(8,128)(2,1)}, bf16[512,4352]{1,0:T(8,128)(2,1)S(1)}, u32[]{:S(2)}) copy-start(bf16[512,4352]{1,0:T(8,128)(2,1)S(1)} %get-tuple-element.95) | copy-start | bytes 13369348
  497.8 74.6 %collective-permute-start.1 = (bf16[1,512,1088]{1,2,0:T(8,128)(2,1)}, bf16[1,512,1088]{1,2,0:T(8,128)(2,1)}, u32[]{:S(2)}, u32[]{:S(2)}) collective-permute-start(bf16[1,512,1088]{1,2,0:T(8,128)(2,1)} %slice.217), channel_id=1, source_target_pairs={{1,0},{3,2},{5,4},{7,6},{9,8},{11,10},{13,12},{15,14},{17,16},{19,... | collective-permute-start | bytes 3342344 | tf_op jit(solution)/shard_map/ppermute | solution.py:282
  508.9 6.0 copy-start.11
  518.6 9.4 %copy-start.16 = (bf16[512,16,72]{0,2,1:T(8,128)(2,1)S(1)}, bf16[512,16,72]{0,2,1:T(8,128)(2,1)}, u32[]{:S(2)}) copy-start(bf16[512,16,72]{0,2,1:T(8,128)(2,1)} %pad.74) | copy-start | bytes 3538948
  518.6 9.4 %copy-start.18 = (bf16[512,16,72]{0,2,1:T(8,128)(2,1)S(1)}, bf16[512,16,72]{0,2,1:T(8,128)(2,1)}, u32[]{:S(2)}) copy-start(bf16[512,16,72]{0,2,1:T(8,128)(2,1)} %copy-done.17) | copy-start | bytes 3538948
  529.2 7.3 copy-start.23
  529.2 11.1 %copy-start.35 = (bf16[512,8,1,72]{0,3,2,1:T(8,128)(2,1)}, bf16[512,8,1,72]{0,3,2,1:T(8,128)(2,1)S(1)}, u32[]{:S(2)}) copy-start(bf16[512,8,1,72]{0,3,2,1:T(8,128)(2,1)S(1)} %get-tuple-element.98) | copy-start | bytes 1769476
  533.2 217.2 %collective-permute-start.15 = (bf16[576,2176]{1,0:T(8,128)(2,1)}, bf16[576,2176]{1,0:T(8,128)(2,1)}, u32[]{:S(2)}, u32[]{:S(2)}) collective-permute-start(bf16[576,2176]{1,0:T(8,128)(2,1)} %convolution_convert_fusion), channel_id=1, source_target_pairs={{0,2},{2,0},{4,6},{6,4},{8,10},{10,8},{12,14},{14,12},{16,18},{18,... | collective-permute-start | bytes 7520264 | tf_op jit(solution)/shard_map/ppermute | solution.py:143
  536.5 5.3 copy-start.6
  536.5 5.3 copy-start.58
  541.8 13.9 %copy-start.36 = (bf16[512,8,1,72]{0,3,2,1:T(8,128)(2,1)S(1)}, bf16[512,8,1,72]{0,3,2,1:T(8,128)(2,1)}, u32[]{:S(2)}) copy-start(bf16[512,8,1,72]{0,3,2,1:T(8,128)(2,1)} %copy-done.35) | copy-start | bytes 1769476
  562.0 30.4 %collective-permute-start = (bf16[1,512,1088]{1,2,0:T(8,128)(2,1)}, bf16[1,512,1088]{1,2,0:T(8,128)(2,1)}, u32[]{:S(2)}, u32[]{:S(2)}) collective-permute-start(bf16[1,512,1088]{1,2,0:T(8,128)(2,1)} %slice.215), channel_id=1, source_target_pairs={{1,0},{3,2},{5,4},{7,6},{9,8},{11,10},{13,12},{15,14},{17,16},{19,... | collective-permute-start | bytes 3342344 | tf_op jit(solution)/shard_map/ppermute | solution.py:282
  563.3 71.6 %collective-permute-start.21 = (bf16[2176,544]{0,1:T(8,128)(2,1)}, bf16[2176,544]{0,1:T(8,128)(2,1)}, u32[]{:S(2)}, u32[]{:S(2)}) collective-permute-start(bf16[2176,544]{0,1:T(8,128)(2,1)} %convolution_convert_fusion.2), channel_id=1, source_target_pairs={{0,2},{2,0},{4,6},{6,4},{8,10},{10,8},{12,14},{14,12},{16,18},{18,... | collective-permute-start | bytes 7102472 | tf_op jit(solution)/shard_map/ppermute | solution.py:143
  563.6 5.7 collective-permute-start.9
  569.3 70.8 %collective-permute-start.8 = (bf16[576,544]{0,1:T(8,128)(2,1)}, bf16[576,544]{0,1:T(8,128)(2,1)}, u32[]{:S(2)}, u32[]{:S(2)}) collective-permute-start(bf16[576,544]{0,1:T(8,128)(2,1)} %convolution_convert_fusion.8), channel_id=1, source_target_pairs={{0,2},{2,0},{4,6},{6,4},{8,10},{10,8},{12,14},{14,12},{16,18},{18,... | collective-permute-start | bytes 1880072 | tf_op jit(solution)/shard_map/ppermute | solution.py:143
  572.4 154.5 %collective-permute-start.10 = (bf16[576,544]{0,1:T(8,128)(2,1)}, bf16[576,544]{0,1:T(8,128)(2,1)}, u32[]{:S(2)}, u32[]{:S(2)}) collective-permute-start(bf16[576,544]{0,1:T(8,128)(2,1)} %add_convert_fusion.6), channel_id=1, source_target_pairs={{0,1},{1,0},{2,3},{3,2},{4,5},{5,4},{6,7},{7,6},{8,9},{9,8},{10,11... | collective-permute-start | bytes 1880072 | tf_op jit(solution)/shard_map/ppermute | solution.py:143
  604.8 5.6 copy-start.37
  614.6 6.7 copy-start.7
  614.6 6.7 copy-start.45
  614.6 6.7 copy-start.50
  614.6 6.7 copy-start.53
  614.6 130.0 %collective-permute-start.3 = (bf16[576,1632]{1,0:T(8,128)(2,1)}, bf16[576,1632]{1,0:T(8,128)(2,1)}, u32[]{:S(2)}, u32[]{:S(2)}) collective-permute-start(bf16[576,1632]{1,0:T(8,128)(2,1)} %convolution_convert_fusion.4), channel_id=1, source_target_pairs={{0,2},{2,0},{4,6},{6,4},{8,10},{10,8},{12,14},{14,12},{16,18},{18,... | collective-permute-start | bytes 5640200 | tf_op jit(solution)/shard_map/ppermute | solution.py:143
  634.9 122.0 %collective-permute-start.20 = (bf16[2176,544]{0,1:T(8,128)(2,1)}, bf16[2176,544]{0,1:T(8,128)(2,1)}, u32[]{:S(2)}, u32[]{:S(2)}) collective-permute-start(bf16[2176,544]{0,1:T(8,128)(2,1)} %convolution_convert_fusion.3), channel_id=1, source_target_pairs={{0,2},{2,0},{4,6},{6,4},{8,10},{10,8},{12,14},{14,12},{16,18},{18,... | collective-permute-start | bytes 7102472 | tf_op jit(solution)/shard_map/ppermute | solution.py:143
  640.1 117.3 %collective-permute-start.22 = (bf16[2176,544]{0,1:T(8,128)(2,1)}, bf16[2176,544]{0,1:T(8,128)(2,1)}, u32[]{:S(2)}, u32[]{:S(2)}) collective-permute-start(bf16[2176,544]{0,1:T(8,128)(2,1)} %add_convert_fusion.1), channel_id=1, source_target_pairs={{0,1},{1,0},{2,3},{3,2},{4,5},{5,4},{6,7},{7,6},{8,9},{9,8},{10,11... | collective-permute-start | bytes 7102472 | tf_op jit(solution)/shard_map/ppermute | solution.py:143
  730.0 6.7 copy-start.15
  734.3 10.1 %collective-permute-start.11 = (bf16[4,72,544]{2,1,0:T(8,128)(2,1)S(1)}, bf16[4,72,544]{2,1,0:T(8,128)(2,1)S(1)}, u32[]{:S(2)}, u32[]{:S(2)}) collective-permute-start(bf16[4,72,544]{2,1,0:T(8,128)(2,1)S(1)} %fusion.76), channel_id=1, source_target_pairs={{0,4},{2,6},{4,0},{6,2},{8,12},{10,14},{12,8},{14,10},{16,20},{18,... | collective-permute-start | bytes 940040 | tf_op jit(solution)/shard_map/ppermute | solution.py:143
  736.6 7.8 copy-start.20
  736.6 9.4 %copy-start.25 = (bf16[512,8,1,72]{0,3,2,1:T(8,128)(2,1)S(1)}, bf16[512,8,1,72]{0,3,2,1:T(8,128)(2,1)}, u32[]{:S(2)}) copy-start(bf16[512,8,1,72]{0,3,2,1:T(8,128)(2,1)} %get-tuple-element.80) | copy-start | bytes 1769476
  744.4 28.1 %collective-permute-start.2 = (bf16[576,1632]{1,0:T(8,128)(2,1)}, bf16[576,1632]{1,0:T(8,128)(2,1)}, u32[]{:S(2)}, u32[]{:S(2)}) collective-permute-start(bf16[576,1632]{1,0:T(8,128)(2,1)} %convolution_convert_fusion.5), channel_id=1, source_target_pairs={{0,2},{2,0},{4,6},{6,4},{8,10},{10,8},{12,14},{14,12},{16,18},{18,... | collective-permute-start | bytes 5640200 | tf_op jit(solution)/shard_map/ppermute | solution.py:143
  744.5 7.6 slice-start.8
  744.6 7.6 slice-start.9
  744.6 7.6 copy-start.24
  744.6 12.3 %collective-permute-start.12 = (bf16[2,72,544]{2,1,0:T(8,128)(2,1)S(1)}, bf16[2,72,544]{2,1,0:T(8,128)(2,1)S(1)}, u32[]{:S(2)}, u32[]{:S(2)}) collective-permute-start(bf16[2,72,544]{2,1,0:T(8,128)(2,1)S(1)} %fusion.77), channel_id=1, source_target_pairs={{0,8},{2,10},{4,12},{6,14},{8,0},{10,2},{12,4},{14,6},{16,24},{18,... | collective-permute-start | bytes 470024 | tf_op jit(solution)/shard_map/ppermute | solution.py:143
  746.1 12.8 %slice-start.4 = ((s8[4734976]{0:T(1024)(128)(4,1)}), s8[4194304]{0:T(1024)(128)(4,1)S(1)}, s32[]{:S(2)}) async-start(s8[4734976]{0:T(1024)(128)(4,1)} %bitcast.246), calls=%async_computation.8 | async-start | bytes 8388608
  750.4 8.5 slice-start.5
  750.4 44.9 %collective-permute-start.4 = (bf16[576,1632]{1,0:T(8,128)(2,1)}, bf16[576,1632]{1,0:T(8,128)(2,1)}, u32[]{:S(2)}, u32[]{:S(2)}) collective-permute-start(bf16[576,1632]{1,0:T(8,128)(2,1)} %add_convert_fusion.2), channel_id=1, source_target_pairs={{0,1},{1,0},{2,3},{3,2},{4,5},{5,4},{6,7},{7,6},{8,9},{9,8},{10,11... | collective-permute-start | bytes 5640200 | tf_op jit(solution)/shard_map/ppermute | solution.py:143
  756.9 45.0 %collective-permute-start.14 = (bf16[576,2176]{1,0:T(8,128)(2,1)}, bf16[576,2176]{1,0:T(8,128)(2,1)S(1)}, u32[]{:S(2)}, u32[]{:S(2)}) collective-permute-start(bf16[576,2176]{1,0:T(8,128)(2,1)} %convolution_convert_fusion.1), channel_id=1, source_target_pairs={{0,2},{2,0},{4,6},{6,4},{8,10},{10,8},{12,14},{14,12},{16,18},{18,... | collective-permute-start | bytes 7520264 | tf_op jit(solution)/shard_map/ppermute | solution.py:143
  756.9 91.5 %collective-permute-start.16 = (bf16[576,2176]{1,0:T(8,128)(2,1)}, bf16[576,2176]{1,0:T(8,128)(2,1)}, u32[]{:S(2)}, u32[]{:S(2)}) collective-permute-start(bf16[576,2176]{1,0:T(8,128)(2,1)} %add_convert_fusion), channel_id=1, source_target_pairs={{0,1},{1,0},{2,3},{3,2},{4,5},{5,4},{6,7},{7,6},{8,9},{9,8},{10,11... | collective-permute-start | bytes 7520264 | tf_op jit(solution)/shard_map/ppermute | solution.py:143
  757.4 95.4 %collective-permute-start.13 = (bf16[1,72,544]{2,1,0:T(8,128)(2,1)S(1)}, bf16[1,72,544]{2,1,0:T(8,128)(2,1)S(1)}, u32[]{:S(2)}, u32[]{:S(2)}) collective-permute-start(bf16[1,72,544]{2,1,0:T(8,128)(2,1)S(1)} %dynamic-slice_convert_fusion.9), channel_id=1, source_target_pairs={{0,16},{2,18},{4,20},{6,22},{8,24},{10,26},{12,28},{14,30},{16,0},... | collective-permute-start | bytes 235016 | tf_op jit(solution)/shard_map/ppermute | solution.py:143
  770.4 78.0 %slice-start.2 = ((s8[5013504]{0:T(1024)(128)(4,1)}), s8[4194304]{0:T(1024)(128)(4,1)S(1)}, s32[]{:S(2)}) async-start(s8[5013504]{0:T(1024)(128)(4,1)} %bitcast.242), calls=%async_computation.6 | async-start | bytes 8388608
  772.5 75.9 %slice-start.3 = ((s8[5013504]{0:T(1024)(128)(4,1)}), s8[819200]{0:T(1024)(128)(4,1)S(1)}, s32[]{:S(2)}) async-start(s8[5013504]{0:T(1024)(128)(4,1)} %bitcast.242), calls=%async_computation.7 | async-start | bytes 1638400
  772.5 81.8 %collective-permute-start.23 = (bf16[4,272,544]{2,1,0:T(8,128)(2,1)S(1)}, bf16[4,272,544]{2,1,0:T(8,128)(2,1)S(1)}, u32[]{:S(2)}, u32[]{:S(2)}) collective-permute-start(bf16[4,272,544]{2,1,0:T(8,128)(2,1)S(1)} %fusion.39), channel_id=1, source_target_pairs={{0,4},{2,6},{4,0},{6,2},{8,12},{10,14},{12,8},{14,10},{16,20},{18,... | collective-permute-start | bytes 3551240 | tf_op jit(solution)/shard_map/ppermute | solution.py:143
  799.0 55.3 %slice-start.6 = ((s8[5570560]{0:T(1024)(128)(4,1)}), s8[4194304]{0:T(1024)(128)(4,1)S(1)}, s32[]{:S(2)}) async-start(s8[5570560]{0:T(1024)(128)(4,1)} %bitcast.250), calls=%async_computation.10 | async-start | bytes 8388608
  800.1 54.2 %slice-start.7 = ((s8[5570560]{0:T(1024)(128)(4,1)}), s8[1376256]{0:T(1024)(128)(4,1)S(1)}, s32[]{:S(2)}) async-start(s8[5570560]{0:T(1024)(128)(4,1)} %bitcast.250), calls=%async_computation.11 | async-start | bytes 2752512
  800.1 53.3 %collective-permute-start.5 = (bf16[4,72,1632]{2,1,0:T(8,128)(2,1)}, bf16[4,72,1632]{2,1,0:T(8,128)(2,1)S(1)}, u32[]{:S(2)}, u32[]{:S(2)}) collective-permute-start(bf16[4,72,1632]{2,1,0:T(8,128)(2,1)} %fusion.44), channel_id=1, source_target_pairs={{0,4},{2,6},{4,0},{6,2},{8,12},{10,14},{12,8},{14,10},{16,20},{18,... | collective-permute-start | bytes 2820104 | tf_op jit(solution)/shard_map/ppermute | solution.py:143
  850.9 29.0 %collective-permute-start.17 = (bf16[4,72,2176]{2,1,0:T(8,128)(2,1)S(1)}, bf16[4,72,2176]{2,1,0:T(8,128)(2,1)S(1)}, u32[]{:S(2)}, u32[]{:S(2)}) collective-permute-start(bf16[4,72,2176]{2,1,0:T(8,128)(2,1)S(1)} %fusion.40), channel_id=1, source_target_pairs={{0,4},{2,6},{4,0},{6,2},{8,12},{10,14},{12,8},{14,10},{16,20},{18,... | collective-permute-start | bytes 3760136 | tf_op jit(solution)/shard_map/ppermute | solution.py:143
  853.7 27.1 %collective-permute-start.6 = (bf16[2,72,1632]{2,1,0:T(8,128)(2,1)S(1)}, bf16[2,72,1632]{2,1,0:T(8,128)(2,1)S(1)}, u32[]{:S(2)}, u32[]{:S(2)}) collective-permute-start(bf16[2,72,1632]{2,1,0:T(8,128)(2,1)S(1)} %fusion.74), channel_id=1, source_target_pairs={{0,8},{2,10},{4,12},{6,14},{8,0},{10,2},{12,4},{14,6},{16,24},{18,... | collective-permute-start | bytes 1410056 | tf_op jit(solution)/shard_map/ppermute | solution.py:143
  854.7 27.7 %collective-permute-start.24 = (bf16[2,272,544]{2,1,0:T(8,128)(2,1)S(1)}, bf16[2,272,544]{2,1,0:T(8,128)(2,1)S(1)}, u32[]{:S(2)}, u32[]{:S(2)}) collective-permute-start(bf16[2,272,544]{2,1,0:T(8,128)(2,1)S(1)} %fusion.47), channel_id=1, source_target_pairs={{0,8},{2,10},{4,12},{6,14},{8,0},{10,2},{12,4},{14,6},{16,24},{18,... | collective-permute-start | bytes 1775624 | tf_op jit(solution)/shard_map/ppermute | solution.py:143
  880.3 27.3 %collective-permute-start.18 = (bf16[2,72,2176]{2,1,0:T(8,128)(2,1)S(1)}, bf16[2,72,2176]{2,1,0:T(8,128)(2,1)S(1)}, u32[]{:S(2)}, u32[]{:S(2)}) collective-permute-start(bf16[2,72,2176]{2,1,0:T(8,128)(2,1)S(1)} %fusion.48), channel_id=1, source_target_pairs={{0,8},{2,10},{4,12},{6,14},{8,0},{10,2},{12,4},{14,6},{16,24},{18,... | collective-permute-start | bytes 1880072 | tf_op jit(solution)/shard_map/ppermute | solution.py:143
  880.9 27.0 %collective-permute-start.7 = (bf16[1,72,1632]{2,1,0:T(8,128)(2,1)S(1)}, bf16[1,72,1632]{2,1,0:T(8,128)(2,1)S(1)}, u32[]{:S(2)}, u32[]{:S(2)}) collective-permute-start(bf16[1,72,1632]{2,1,0:T(8,128)(2,1)S(1)} %dynamic-slice_convert_fusion.7), channel_id=1, source_target_pairs={{0,16},{2,18},{4,20},{6,22},{8,24},{10,26},{12,28},{14,30},{16,0},... | collective-permute-start | bytes 705032 | tf_op jit(solution)/shard_map/ppermute | solution.py:143
  882.7 26.0 %collective-permute-start.25 = (bf16[1,272,544]{2,1,0:T(8,128)(2,1)S(1)}, bf16[1,272,544]{2,1,0:T(8,128)(2,1)S(1)}, u32[]{:S(2)}, u32[]{:S(2)}) collective-permute-start(bf16[1,272,544]{2,1,0:T(8,128)(2,1)S(1)} %dynamic-slice_convert_fusion.5), channel_id=1, source_target_pairs={{0,16},{2,18},{4,20},{6,22},{8,24},{10,26},{12,28},{14,30},{16,0},... | collective-permute-start | bytes 887816 | tf_op jit(solution)/shard_map/ppermute | solution.py:143
  907.8 14.8 %collective-permute-start.19 = (bf16[1,72,2176]{2,1,0:T(8,128)(2,1)S(1)}, bf16[1,72,2176]{2,1,0:T(8,128)(2,1)S(1)}, u32[]{:S(2)}, u32[]{:S(2)}) collective-permute-start(bf16[1,72,2176]{2,1,0:T(8,128)(2,1)S(1)} %dynamic-slice_convert_fusion.6), channel_id=1, source_target_pairs={{0,16},{2,18},{4,20},{6,22},{8,24},{10,26},{12,28},{14,30},{16,0},... | collective-permute-start | bytes 940040 | tf_op jit(solution)/shard_map/ppermute | solution.py:143
  (38 other events, 102.2 us)
Sparse Core Ops, SparseCore 0:
  91.9 44.3 all-gather.10
  139.0 66.6 all-gather.8
  208.4 99.7 all-gather.12
  310.8 83.2 all-gather.14
